TPU v7x, 512 devices: a whole 4x8x8 slice. The times are simulated.
512 devices in a mesh: img: 32 (over y_hi, x, core), cap: 16 (over y_lo, z).
Axes of the slice: x: 4, y: 8 (y_hi: 4, y_lo: 2; y = y_hi * 2 + y_lo), z: 8, core: 2. Of those that a mesh axis runs over, the one named last changes fastest.
Arguments:
- image_student: bfloat16 [10240, 1024], P(('img', 'cap')), may hold values from -64 to 64
- caption_student: bfloat16 [10240, 1024], P(('cap', 'img')), may hold values from -64 to 64
- image_teacher: bfloat16 [10240, 768], P(('img', 'cap')), may hold values from -64 to 64
- caption_teacher: bfloat16 [10240, 768], P(('cap', 'img')), may hold values from -64 to 64
Outputs:
- image_grad: float32 [10240, 1024], P(('img', 'cap'))
- caption_grad: float32 [10240, 1024], P(('cap', 'img'))
All inputs are finite; a program needn't handle non-finite values.
Results may differ from a plain program's by a relative error of at most 0.004.
Values may be sent and summed in bfloat16 or wider, within the bound.
A program may use at most 64 MiB of HBM per device.

v0:
```python
import math

import jax
import jax.numpy as jnp
from jax import lax
from jax.sharding import PartitionSpec as P

logit_gain = 3.0


def scores(left, right, factor):
    return factor * lax.dot_general(
        left, right, (((1,), (1,)), ((), ())), preferred_element_type=jnp.float32
    )


def partials(student, teacher, reduce_dim):
    result = []
    for matrix in (student, teacher):
        peak = jnp.max(matrix, axis=reduce_dim)
        total = jnp.sum(jnp.exp(matrix - jnp.expand_dims(peak, reduce_dim)), axis=reduce_dim)
        result.append(peak)
        result.append(total)
    return tuple(result)


def row_pool(parts):
    peak_s, peak_t = lax.pmax((parts[0], parts[2]), "cap")
    total_s, total_t = lax.psum(
        (parts[1] * jnp.exp(parts[0] - peak_s), parts[3] * jnp.exp(parts[2] - peak_t)), "cap"
    )
    return (peak_s + jnp.log(total_s), peak_t + jnp.log(total_t))


def column_pool(parts):
    peak_s, peak_t = lax.pmax((parts[0], parts[2]), "img")
    total_s, total_t = lax.psum(
        (parts[1] * jnp.exp(parts[0] - peak_s), parts[3] * jnp.exp(parts[2] - peak_t)), "img"
    )
    return (peak_s + jnp.log(total_s), peak_t + jnp.log(total_t))


def diagonal(row_offset, col_offset, row_count, col_count):
    row_ids = row_offset + jnp.arange(row_count, dtype=jnp.int32)
    col_ids = col_offset + jnp.arange(col_count, dtype=jnp.int32)
    return (row_ids[:, None] == col_ids[None, :]).astype(jnp.float32)


def grad_tile(student, teacher, row_student, row_teacher, col_student, col_teacher, diag_mask):
    tile_grad = 0.5 * (
        jnp.exp(student - row_student[:, None]) + jnp.exp(student - col_student[None, :])
    )
    tile_grad = tile_grad - 0.25 * (
        jnp.exp(teacher - row_teacher[:, None]) + jnp.exp(teacher - col_teacher[None, :])
    )
    return (tile_grad - 0.5 * diag_mask).astype(jnp.bfloat16)


def local(image_student, caption_student, image_teacher, caption_teacher):
    img_student, img_teacher = (
        lax.all_gather(image_student, "cap", axis=0, tiled=True),
        lax.all_gather(image_teacher, "cap", axis=0, tiled=True),
    )
    row_count = img_student.shape[0]
    width = img_student.shape[1]
    student_gain = logit_gain / math.sqrt(width)
    teacher_gain = logit_gain / math.sqrt(img_teacher.shape[1])
    row_offset = lax.axis_index("img") * row_count
    cap_student, cap_teacher = (
        lax.all_gather(caption_student, "img", axis=0, tiled=True),
        lax.all_gather(caption_teacher, "img", axis=0, tiled=True),
    )
    col_count = cap_student.shape[0]
    col_offset = lax.axis_index("cap") * col_count
    student = scores(img_student, cap_student, student_gain)
    teacher = scores(img_teacher, cap_teacher, teacher_gain)
    row_student, row_teacher = row_pool(partials(student, teacher, 1))
    col_student, col_teacher = column_pool(partials(student, teacher, 0))
    diag_mask = diagonal(row_offset, col_offset, row_count, col_count)
    tile_grad = grad_tile(
        student, teacher, row_student, row_teacher, col_student, col_teacher, diag_mask
    )
    portion = tile_grad
    image_grad = lax.psum_scatter(
        jnp.dot(portion, cap_student, preferred_element_type=jnp.float32),
        "cap",
        scatter_dimension=0,
        tiled=True,
    )
    portion = tile_grad
    caption_grad = lax.psum_scatter(
        lax.dot_general(
            portion, img_student, (((0,), (0,)), ((), ())), preferred_element_type=jnp.float32
        ),
        "img",
        scatter_dimension=0,
        tiled=True,
    )
    return (image_grad, caption_grad)


def solution(mesh):
    return jax.shard_map(
        local,
        mesh=mesh,
        in_specs=(
            P(("img", "cap"), None),
            P(("cap", "img"), None),
            P(("img", "cap"), None),
            P(("cap", "img"), None),
        ),
        out_specs=(P(("img", "cap"), None), P(("cap", "img"), None)),
        check_vma=False,
    )
```

profile of v0, /device:TPU:1, one launch (start us, length us, event | category | flops | bytes accessed | tf_op | source)
XLA Modules:
  0.0 520.7 jit_solution(7453703374014174112)
XLA Ops:
  7.2 0.0 all-gather.6.cloned.1.call-start
  7.2 0.7 all-gather.6.cloned.1.call-update
  7.9 37.4 %all-gather.2 = bf16[16,20,768]{2,1,0:T(8,128)(2,1)S(1)} all-gather(bf16[1,20,768]{2,1,0:T(8,128)(2,1)} %bitcast.20), channel_id=1, replica_groups=mesh['img'=32,'cap'=16] {'cap'}, dimensions={0}, use_global_device_ids=true | all-gather | bytes 522240 | tf_op jit(solution)/shard_map/all_gather | solution.py:62
  45.3 0.9 reshape.25
  46.2 58.1 %all-gather.3 = bf16[32,20,768]{2,1,0:T(8,128)(2,1)S(1)} all-gather(bf16[1,20,768]{2,1,0:T(8,128)(2,1)S(1)} %bitcast.21), channel_id=1, replica_groups=mesh['img'=32,'cap'=16] {'img'}, dimensions={0}, use_global_device_ids=true | all-gather | bytes 1013760 | tf_op jit(solution)/shard_map/all_gather | solution.py:71
  104.2 0.2 reshape.27
  104.5 0.6 copy-done.2
  105.0 27.7 %all-gather = bf16[16,20,1024]{2,1,0:T(8,128)(2,1)S(1)} all-gather(bf16[1,20,1024]{2,1,0:T(8,128)(2,1)S(1)} %bitcast.18), channel_id=1, replica_groups=mesh['img'=32,'cap'=16] {'cap'}, dimensions={0}, use_global_device_ids=true | all-gather | bytes 696320 | tf_op jit(solution)/shard_map/all_gather | solution.py:61
  132.7 1.0 reshape.21
  133.7 0.7 fusion.3
  134.4 0.3 exponential_reduce_fusion.1
  134.7 0.0 all-gather.6.cloned.1.call-done
  134.8 2.3 reshape.23
  137.1 1.9 fusion.2
  139.0 76.9 %all-reduce.5 = (f32[640]{0:T(1024)S(1)}, f32[640]{0:T(1024)S(1)}) all-reduce(f32[640]{0:T(1024)S(1)} %get-tuple-element.9, f32[640]{0:T(1024)S(1)} %get-tuple-element.5), channel_id=1, replica_groups=mesh['img'=32,'cap'=16] {'img'}, use_global_device_ids=true, to_apply=%region_13.0 | all-reduce | flops 1280 | bytes 10240 | tf_op jit(solution)/shard_map/pmax | solution.py:36
  215.9 25.3 %all-reduce.7 = (f32[320]{0:T(512)S(1)}, f32[320]{0:T(512)S(1)}) all-reduce(f32[320]{0:T(512)S(1)} %get-tuple-element.8, f32[320]{0:T(512)S(1)} %get-tuple-element.4), channel_id=1, replica_groups=mesh['img'=32,'cap'=16] {'cap'}, use_global_device_ids=true, to_apply=%region_9.0 | all-reduce | flops 640 | bytes 5120 | tf_op jit(solution)/shard_map/pmax | solution.py:28
  241.2 0.3 exponential_reduce_fusion.3
  241.5 77.9 %all-reduce.4 = (f32[640]{0:T(1024)S(1)}, f32[640]{0:T(1024)S(1)}) all-reduce(f32[640]{0:T(1024)S(1)} %exponential_multiply_fusion, f32[640]{0:T(1024)S(1)} %exponential_multiply_fusion.1), channel_id=1, replica_groups=mesh['img'=32,'cap'=16] {'img'}, use_global_device_ids=true, to_apply=%region_15.0 | all-reduce | flops 1280 | bytes 10240 | tf_op jit(solution)/shard_map/psum | solution.py:37
  319.5 23.9 %all-reduce.6 = (f32[320]{0:T(512)S(1)}, f32[320]{0:T(512)S(1)}) all-reduce(f32[320]{0:T(512)S(1)} %exponential_multiply_fusion.2, f32[320]{0:T(512)S(1)} %exponential_multiply_fusion.3), channel_id=1, replica_groups=mesh['img'=32,'cap'=16] {'cap'}, use_global_device_ids=true, to_apply=%region_11.0 | all-reduce | flops 640 | bytes 5120 | tf_op jit(solution)/shard_map/psum | solution.py:29
  343.4 1.8 subtract_convert_fusion
  345.2 0.7 fusion.4
  345.9 34.1 %fusion = f32[24,1024]{1,0:T(8,128)S(1)} fusion(f32[320,1024]{1,0:T(8,128)S(1)} %fusion.4), kind=kCustom, calls=%all-reduce-scatter | all-reduce-scatter fusion | flops 393217 | bytes 1411072
  380.1 1.3 collective-permute-start.1
  381.4 3.2 collective-permute-start
  384.5 2.0 fusion.5
  386.5 1.8 collective-permute-start.2
  388.3 99.2 %fusion.1 = f32[24,1024]{1,0:T(8,128)S(1)} fusion(f32[640,1024]{1,0:T(8,128)S(1)} %fusion.5), kind=kCustom, calls=%all-reduce-scatter.1 | all-reduce-scatter fusion | flops 786433 | bytes 2721792
  487.5 1.3 collective-permute-start.8
  488.8 1.3 dynamic-slice.6
  490.1 1.3 dynamic-slice.10
  492.7 1.3 collective-permute-start.7
  494.0 0.0 collective-permute-done.2
  494.0 8.7 %collective-permute-start.6 = (f32[24,1024]{1,0:T(8,128)S(1)}, f32[24,1024]{1,0:T(8,128)S(1)}, u32[]{:S(2)}, u32[]{:S(2)}) collective-permute-start(f32[24,1024]{1,0:T(8,128)S(1)} %fusion.1), channel_id=1, source_target_pairs={{0,64},{16,80},{32,96},{48,112},{64,128},{80,144},{96,160},{112,17... | collective-permute-start | bytes 294920
  502.6 0.0 collective-permute-done.1
  502.6 1.3 collective-permute-start.5
  504.0 0.0 collective-permute-done
  504.0 4.0 collective-permute-start.4
  508.0 0.5 concatenate
  508.4 0.0 collective-permute-done.8
  508.5 2.2 collective-permute-start.3
  510.7 0.7 constant_dynamic-slice_fusion.1
  511.3 0.0 collective-permute-done.7
  511.3 0.0 collective-permute-done.6
  511.3 0.0 collective-permute-done.5
  511.3 0.0 collective-permute-done.4
  511.3 0.9 collective-permute-done.3
  512.3 0.9 concatenate.1
  513.2 0.7 constant_dynamic-slice_fusion
  (17 shorter events, 0.1 us)
Async XLA Ops:
  7.2 39.0 %copy-start.3 = (bf16[20,768]{1,0:T(8,128)(2,1)S(1)}, bf16[20,768]{1,0:T(8,128)(2,1)}, u32[]{:S(2)}) copy-start(bf16[20,768]{1,0:T(8,128)(2,1)} %param.7) | copy-start | bytes 92164
  7.2 127.6 %all-gather.6.cloned.1.call-start = ((), (), s32[]{:S(2)}) async-start(), calls=%async_computation | async-start | bytes 1622016 | tf_op jit(solution)/shard_map/all_gather | solution.py:70
  104.2 0.8 copy-start.2
  104.5 29.3 %copy-start.1 = (bf16[320,768]{1,0:T(8,128)(2,1)S(1)}, bf16[320,768]{1,0:T(8,128)(2,1)}, u32[]{:S(2)}) copy-start(bf16[320,768]{1,0:T(8,128)(2,1)} %reshape.25) | copy-start | bytes 1474564
  139.0 204.5 %copy-start = (f32[320,640]{1,0:T(8,128)}, f32[320,640]{1,0:T(8,128)S(1)}, u32[]{:S(2)}) copy-start(f32[320,640]{1,0:T(8,128)S(1)} %get-tuple-element.19) | copy-start | bytes 2457604
  380.1 122.6 %collective-permute-start.1 = (f32[24,1024]{1,0:T(8,128)S(1)}, f32[24,1024]{1,0:T(8,128)S(1)}, u32[]{:S(2)}, u32[]{:S(2)}) collective-permute-start(f32[24,1024]{1,0:T(8,128)S(1)} %fusion), channel_id=1, source_target_pairs={{0,2},{1,3},{2,4},{3,5},{4,6},{5,7},{6,8},{7,9},{8,10},{9,11},{10,... | collective-permute-start | bytes 294920
  381.4 122.6 %collective-permute-start = (f32[24,1024]{1,0:T(8,128)S(1)}, f32[24,1024]{1,0:T(8,128)S(1)}, u32[]{:S(2)}, u32[]{:S(2)}) collective-permute-start(f32[24,1024]{1,0:T(8,128)S(1)} %fusion), channel_id=1, source_target_pairs={{0,1},{1,2},{2,3},{3,4},{4,5},{5,6},{6,7},{7,8},{8,9},{9,10},{10,1... | collective-permute-start | bytes 294920
  386.5 107.5 %collective-permute-start.2 = (f32[12,1024]{1,0:T(8,128)S(1)}, f32[12,1024]{1,0:T(8,128)S(1)}, u32[]{:S(2)}, u32[]{:S(2)}) collective-permute-start(f32[12,1024]{1,0:T(8,128)S(1)} %slice), channel_id=1, source_target_pairs={{0,3},{1,4},{2,5},{3,6},{4,7},{5,8},{6,9},{7,10},{8,11},{9,12},{10... | collective-permute-start | bytes 147464
  487.5 20.9 %collective-permute-start.8 = (f32[4,1024]{1,0:T(4,128)S(1)}, f32[4,1024]{1,0:T(4,128)S(1)}, u32[]{:S(2)}, u32[]{:S(2)}) collective-permute-start(f32[4,1024]{1,0:T(4,128)S(1)} %slice.1), channel_id=1, source_target_pairs={{0,96},{16,112},{32,128},{48,144},{64,160},{80,176},{96,192},{112,... | collective-permute-start | bytes 49160
  492.7 18.7 %collective-permute-start.7 = (f32[24,1024]{1,0:T(8,128)S(1)}, f32[24,1024]{1,0:T(8,128)S(1)}, u32[]{:S(2)}, u32[]{:S(2)}) collective-permute-start(f32[24,1024]{1,0:T(8,128)S(1)} %fusion.1), channel_id=1, source_target_pairs={{0,80},{16,96},{32,112},{48,128},{64,144},{80,160},{96,176},{112,1... | collective-permute-start | bytes 294920
  494.0 17.4 %collective-permute-start.6 = (f32[24,1024]{1,0:T(8,128)S(1)}, f32[24,1024]{1,0:T(8,128)S(1)}, u32[]{:S(2)}, u32[]{:S(2)}) collective-permute-start(f32[24,1024]{1,0:T(8,128)S(1)} %fusion.1), channel_id=1, source_target_pairs={{0,64},{16,80},{32,96},{48,112},{64,128},{80,144},{96,160},{112,17... | collective-permute-start | bytes 294920
  502.6 8.7 %collective-permute-start.5 = (f32[24,1024]{1,0:T(8,128)S(1)}, f32[24,1024]{1,0:T(8,128)S(1)}, u32[]{:S(2)}, u32[]{:S(2)}) collective-permute-start(f32[24,1024]{1,0:T(8,128)S(1)} %fusion.1), channel_id=1, source_target_pairs={{0,48},{16,64},{32,80},{48,96},{64,112},{80,128},{96,144},{112,160... | collective-permute-start | bytes 294920
  504.0 7.4 %collective-permute-start.4 = (f32[24,1024]{1,0:T(8,128)S(1)}, f32[24,1024]{1,0:T(8,128)S(1)}, u32[]{:S(2)}, u32[]{:S(2)}) collective-permute-start(f32[24,1024]{1,0:T(8,128)S(1)} %fusion.1), channel_id=1, source_target_pairs={{0,32},{16,48},{32,64},{48,80},{64,96},{80,112},{96,128},{112,144}... | collective-permute-start | bytes 294920
  508.5 3.8 collective-permute-start.3
Sparse Core Ops, SparseCore 0:
  11.1 66.0 all-gather.5
where the time goes:
time: 530 us; the launch traced here: 521 us
  blocking collectives  460 us (87%)
  starting transfers between devices  25 us (5%)
  between operations  15.6 us (3%)
  local copies, waits for them, and re-layouts  10.2 us (2%)
    unnamed x2, blocking collectives  133 us
    psum x1, blocking collectives, column_pool(): lax.psum((parts[1] * jnp.exp(parts[0] - peak_s), parts[3] * jnp.exp(parts...  77.9 us
    pmax x1, blocking collectives, column_pool(): peak_s, peak_t = lax.pmax((parts[0], parts[2]), 'img')  76.9 us
    all_gather x1, blocking collectives, local(): lax.all_gather(caption_teacher, 'img', axis=0, tiled=True)  58.1 us
    all_gather x1, blocking collectives, local(): lax.all_gather(image_teacher, 'cap', axis=0, tiled=True)  37.4 us
    all_gather x1, blocking collectives, local(): lax.all_gather(image_student, 'cap', axis=0, tiled=True)  27.7 us
    pmax x1, blocking collectives, row_pool(): peak_s, peak_t = lax.pmax((parts[0], parts[2]), 'cap')  25.3 us
    unnamed x9, starting transfers between devices  25 us
  transfers between devices with their start and end apart: 10, of which 1 were waited for; matrix products, arithmetic and copies ran while one was open for 21% of the time, Pallas kernels for 0%

commit v1 on v0

v1 whole, which is shorter than its diff:
```python
import math

import jax
import jax.numpy as jnp
from jax import lax
from jax.experimental import pallas as pl
from jax.experimental.pallas import tpu as pltpu
from jax.sharding import PartitionSpec as P

MESH = pl.DeviceIdType.MESH
GAIN = 3.0
NX, NYH, NZ = 4, 4, 8
NI, NC = 2 * NZ, 2 * NX * NYH
DS, DT = 1024, 768
W = DS + DT + 512
WG = DS + 256
B = 20
RI, RC = 16 * NI, 16 * NC
MI, MC = 20 * NI, 20 * NC
LI = 384
BF, F32 = jnp.bfloat16, jnp.float32


def dot_t(a, b):
    return lax.dot_general(a, b, (((1,), (1,)), ((), ())), preferred_element_type=F32)


def t_dot(a, b):
    return lax.dot_general(a, b, (((0,), (0,)), ((), ())), preferred_element_type=F32)


def fold_matrix():
    a = lax.broadcasted_iota(jnp.int32, (256, 256), 0)
    b = lax.broadcasted_iota(jnp.int32, (256, 256), 1)
    source = 16 * ((a >> 2) & 15) + 4 * (a >> 6) + (a & 3)
    return jnp.where(b == source, 1.0, 0.0).astype(BF)


def kernel(
    is_ref, cs_ref, it_ref, ct_ref, oi_ref, oc_ref,
    gi, gc, ar, br, rp, es, et, fs, ft, rmx, tb, tb2, rxr, rxc,
    tg, pi, si, ri, pc, sc, r_core, s_x, r_x, s_y, r_y,
    gi_r, gi_s, gc_r, gc_s, lr_r, lr_s, lc_r, lc_s,
    ri_r, ri_s, co_r, co_s, x_r, x_s, y_r, y_s,
):
    img, cap = lax.axis_index("img"), lax.axis_index("cap")
    yh, x, core = img // (2 * NX), (img // 2) % NX, img % 2
    yl, z = cap // NZ, cap % NZ

    def at_img(dyh, dx, dcore):
        return (((yh + dyh) % NYH) * NX + (x + dx) % NX) * 2 + (core + dcore) % 2

    def slot_c(dyh, dx, dcore):
        return ((core + dcore) % 2) * (NX * NYH) + ((x + dx) % NX) * NYH + (yh + dyh) % NYH

    def at_cap(dyl, dz):
        return ((yl + dyl) % 2) * NZ + (z + dz) % NZ

    def remote(src, dst, send, recv, dev):
        return pltpu.make_async_remote_copy(
            src_ref=src, dst_ref=dst, send_sem=send, recv_sem=recv, device_id=dev, device_id_type=MESH
        )

    up, down, pair = (img, at_cap(0, 1)), (img, at_cap(0, -1)), (img, at_cap(1, 0))
    xu, xd, x2 = (at_img(0, 1, 0), cap), (at_img(0, -1, 0), cap), (at_img(0, 2, 0), cap)
    sib = (at_img(0, 0, 1), cap)
    ys = [(at_img(d, 0, 0), cap) for d in (1, 2, 3)]

    barrier = pltpu.get_barrier_semaphore()
    near = [up, down, pair, xu, xd, x2, sib] + ys
    for dev in near:
        pl.semaphore_signal(barrier, inc=1, device_id=dev, device_id_type=MESH)

    me_i, me_c = cap, slot_c(0, 0, 0)
    for s_ref, t_ref, buf, slot in ((is_ref, it_ref, gi, me_i), (cs_ref, ct_ref, gc, me_c)):
        rows = pl.ds(pl.multiple_of(16 * slot, 16), 16)
        buf[rows, 0:DS] = s_ref[0:16, :]
        buf[rows, DS : DS + DT] = t_ref[0:16, :]
        s4 = s_ref[...].astype(F32)[16:20, :]
        t4 = t_ref[...].astype(F32)[16:20, :]
        rp[...] = jnp.zeros_like(rp)
        for q in range(4):
            rp[4 * q : 4 * q + 4, 0:256] = s4[:, 256 * q : 256 * q + 256]
        for q in range(3):
            rp[4 * q : 4 * q + 4, 256:512] = t4[:, 256 * q : 256 * q + 256]
        buf[rows, DS + DT : W] = rp[...].astype(BF)

    pl.semaphore_wait(barrier, len(near))

    pending = []

    def gi_at(slot):
        return gi.at[pl.ds(pl.multiple_of(16 * slot, 16), 16), :]

    def gc_at(slot):
        return gc.at[pl.ds(pl.multiple_of(16 * slot, 16), 16), :]

    count = {"i": 0, "c": 0}

    def send_i(slot, *devs):
        for dev in devs:
            c = remote(gi_at(slot), gi_at(slot), gi_s.at[count["i"]], gi_r.at[slot], dev)
            count["i"] += 1
            c.start()
            pending.append(c)

    def send_c(slot, *devs):
        for dev in devs:
            c = remote(gc_at(slot), gc_at(slot), gc_s.at[count["c"]], gc_r.at[slot], dev)
            count["c"] += 1
            c.start()
            pending.append(c)

    def got_i(slot):
        remote(gi_at(slot), gi_at(slot), gi_s.at[0], gi_r.at[slot], up).wait_recv()

    def got_c(slot):
        remote(gc_at(slot), gc_at(slot), gc_s.at[0], gc_r.at[slot], up).wait_recv()

    def img_own_up(k):
        s = at_cap(0, -k)
        got_i(s)
        if k < 4:
            send_i(s, up)

    def img_own_down(k):
        s = at_cap(0, k)
        got_i(s)
        if k < 3:
            send_i(s, down)

    def img_pair_up(k):
        s = at_cap(1, -k)
        got_i(s)
        if k < 3:
            send_i(s, up)

    def img_pair_down(k):
        s = at_cap(1, k)
        got_i(s)
        if k < 4:
            send_i(s, down)

    def cap_y(j):
        s = slot_c(j, 0, 0)
        got_c(s)
        send_c(s, xu, xd, sib)

    def cap_xu(j):
        s = slot_c(j, -1, 0)
        got_c(s)
        if j < 2:
            send_c(s, xu)
        send_c(s, sib)

    def cap_xd(j):
        s = slot_c(j, 1, 0)
        got_c(s)
        if j >= 2:
            send_c(s, xd)
        send_c(s, sib)

    def cap_x2(j):
        s = slot_c(j, 2, 0)
        got_c(s)
        send_c(s, sib)

    send_i(me_i, pair)
    send_c(me_c, *ys)
    send_i(me_i, up, down)
    send_c(me_c, xu, xd, sib)

    s = at_cap(1, 0)
    got_i(s)
    send_i(s, up, down)
    img_own_up(1)
    img_own_down(1)
    cap_xu(0)
    cap_xd(0)
    cap_y(1)
    cap_y(3)
    img_pair_up(1)
    img_pair_down(1)
    cap_y(2)
    img_own_up(2)
    img_own_down(2)
    cap_xu(1)
    cap_xd(3)
    cap_x2(0)
    img_pair_up(2)
    img_pair_down(2)
    cap_xu(3)
    cap_xd(1)
    img_own_up(3)
    img_own_down(3)
    cap_xu(2)
    cap_xd(2)
    img_pair_up(3)
    img_pair_down(3)
    cap_x2(3)
    cap_x2(1)
    cap_x2(2)
    img_own_up(4)
    img_pair_down(4)
    for dx in range(NX):
        for j in range(NYH):
            got_c(slot_c(j, dx, 1))

    fold = fold_matrix()
    for src, base, dst, off in ((gi, 0, ar, 0), (gc, 0, br, 0), (gc, 256, br, 64)):
        for g, n in ((0, 4), (1, 3)):
            cols = DS + DT + 256 * g
            y = jnp.dot(fold, src[base : base + 256, cols : cols + 256], preferred_element_type=F32).astype(BF)
            for q in range(n):
                c = 256 * (4 * g + q)
                dst[off : off + 64, c : c + 256] = y[64 * q : 64 * q + 64, :]

    row_lse, col_lse, col_max = [], [], []
    for k, (e_row, e_col, lo, width) in enumerate(((es, fs, 0, DS), (et, ft, DS, DT))):
        gain = GAIN / math.sqrt(width)
        cols = slice(lo, lo + width)
        e_col[0:RI, 0:RC] = gain * dot_t(gi[:, cols], gc[:, cols])
        e_col[0:RI, RC:MC] = gain * dot_t(gi[:, cols], br[:, cols])
        e_col[RI:MI, 0:RC] = gain * dot_t(ar[:, cols], gc[:, cols])
        e_col[RI:MI, RC:MC] = gain * dot_t(ar[:, cols], br[:, cols])
        top = None
        lses = []
        for b in range(0, MI, 64):
            blk = e_col[b : b + 64, :]
            m = jnp.max(blk, axis=1, keepdims=True)
            rmx[k, b : b + 64, :] = m
            e = jnp.exp(blk - m)
            e_row[b : b + 64, :] = e
            lses.append(m + jnp.log(jnp.sum(e, axis=1, keepdims=True)))
            t = jnp.max(blk, axis=0, keepdims=True)
            top = t if top is None else jnp.maximum(top, t)
        row_lse.append(lses)
        total = None
        for b in range(0, MI, 64):
            e = jnp.exp(e_col[b : b + 64, :] - top)
            e_col[b : b + 64, :] = e
            t = jnp.sum(e, axis=0, keepdims=True)
            total = t if total is None else total + t
        col_max.append(top)
        col_lse.append(top + jnp.log(total))

    lane = lax.broadcasted_iota(jnp.int32, (64, 128), 1)
    for n, b in enumerate(range(0, MI, 64)):
        tb[b : b + 64, :] = jnp.where(lane == 0, row_lse[0][n], jnp.where(lane == 1, row_lse[1][n], 0.0))
    tb[MI:LI, :] = jnp.zeros((LI - MI, 128), F32)
    rxr[me_i] = tb[...].T[0:2, :]
    rxc[me_c, 0:1, :] = col_lse[0]
    rxc[me_c, 1:2, :] = col_lse[1]

    for j in range(NYH):
        for dx in range(NX):
            for dc in range(2):
                if (j, dx, dc) != (0, 0, 0):
                    n = (j * NX + dx) * 2 + dc
                    c = remote(rxc.at[me_c], rxc.at[me_c], lc_s.at[n], lc_r.at[me_c], (at_img(j, dx, dc), cap))
                    c.start()
                    pending.append(c)
    for dy in range(2):
        for dz in range(NZ):
            if (dy, dz) != (0, 0):
                n = dy * NZ + dz
                c = remote(rxr.at[me_i], rxr.at[me_i], lr_s.at[n], lr_r.at[me_i], (img, at_cap(dy, dz)))
                c.start()
                pending.append(c)
    for dy in range(2):
        for dz in range(NZ):
            if (dy, dz) != (0, 0):
                s = at_cap(dy, dz)
                remote(rxr.at[s], rxr.at[s], lr_s.at[0], lr_r.at[s], up).wait_recv()
    for j in range(NYH):
        for dx in range(NX):
            for dc in range(2):
                if (j, dx, dc) != (0, 0, 0):
                    s = slot_c(j, dx, dc)
                    remote(rxc.at[s], rxc.at[s], lc_s.at[0], lc_r.at[s], up).wait_recv()

    def pool(parts):
        m = jnp.max(parts, axis=0)
        return m + jnp.log(jnp.sum(jnp.exp(parts - m[None]), axis=0))

    tb2[...] = jnp.zeros_like(tb2)
    tb2[0:2, :] = pool(rxr[...])
    rows_all = tb2[...].T
    cols_all = pool(rxc[...])
    f_col_s = 0.5 * jnp.exp(col_max[0] - cols_all[0:1, :])
    f_col_t = 0.25 * jnp.exp(col_max[1] - cols_all[1:2, :])

    b = lax.broadcasted_iota(jnp.int32, (1, MC), 1)
    t = jnp.where(b < RC, b >> 4, (b - RC) >> 2)
    u = jnp.where(b < RC, b & 15, 16 + (b & 3))
    block = (t & 3) * (2 * NX) + ((t >> 2) & 3) * 2 + (t >> 4)
    col_id = cap * MC + block * B + u
    for lo in range(0, MI, 64):
        a = lo + lax.broadcasted_iota(jnp.int32, (64, 1), 0)
        if lo < RI:
            row_id = img * MI + (a >> 4) * B + (a & 15)
        else:
            row_id = img * MI + ((a - RI) >> 2) * B + 16 + (a & 3)
        rows = slice(lo, lo + 64)
        f_row_s = 0.5 * jnp.exp(rmx[0, rows, :] - rows_all[rows, 0:1])
        f_row_t = 0.25 * jnp.exp(rmx[1, rows, :] - rows_all[rows, 1:2])
        g = es[rows, :] * f_row_s + fs[rows, :] * f_col_s
        g = g - (et[rows, :] * f_row_t + ft[rows, :] * f_col_t)
        g = g - jnp.where(row_id == col_id, 0.5, 0.0)
        tg[rows, :] = g.astype(BF)

    pc[...] = t_dot(tg[0:RI, :], gi[:, 0:DS]) + t_dot(tg[RI:MI, :], ar[:, 0:DS])
    for h in range(2):
        rows = slice(256 * h, 256 * h + 256)
        sc[rows, 0:DS] = pc[rows, :]
        rem = jnp.concatenate(
            [pc[RC + 64 * h : RC + 64 * h + 64, 256 * q : 256 * q + 256] for q in range(4)], axis=0
        ).astype(BF)
        sc[rows, DS:WG] = t_dot(fold, rem)
    half = NX * NYH * 16
    core_copies = []
    for n, dx in enumerate((2, 1, 3, 0)):
        there = pl.ds(pl.multiple_of((1 - core) * half + ((x + dx) % NX) * (NYH * 16), 64), 64)
        c = remote(sc.at[there, :], r_core.at[n], co_s.at[n], co_r.at[n], sib)
        c.start()
        core_copies.append(c)
        pending.append(c)

    pi[...] = jnp.dot(tg[:, 0:RC], gc[:, 0:DS], preferred_element_type=F32) + jnp.dot(
        tg[:, RC:MC], br[:, 0:DS], preferred_element_type=F32
    )
    si[:, 0:DS] = pi[0:RI, :].astype(BF)
    rem = jnp.concatenate([pi[RI:MI, 256 * q : 256 * q + 256] for q in range(4)], axis=0).astype(BF)
    si[:, DS:WG] = t_dot(fold, rem).astype(BF)
    for dz in (4, 3, 5, 2, 6, 1, 7, 0):
        for dy in range(2):
            if (dy, dz) != (0, 0):
                n = dy * NZ + dz
                s = at_cap(dy, dz)
                block = si.at[pl.ds(pl.multiple_of(16 * s, 16), 16), :]
                c = remote(block, ri.at[me_i], ri_s.at[n], ri_r.at[me_i], (img, s))
                c.start()
                pending.append(c)

    for n, dx in enumerate((2, 1, 3, 0)):
        here = pl.ds(pl.multiple_of(core * half + ((x + dx) % NX) * (NYH * 16), 64), 64)
        core_copies[n].wait_recv()
        v = sc[here, :] + r_core[n]
        if dx:
            s_x[n] = v.astype(BF)
            dev = (x2, xu, xd)[n]
            c = remote(s_x.at[n], r_x.at[n], x_s.at[n], x_r.at[n], dev)
            c.start()
            pending.append(c)
        else:
            pc[0:64, :] = v[:, 0:DS]
            pc[64:128, 0:256] = v[:, DS:WG]
    for n in range(3):
        remote(r_x.at[n], r_x.at[n], x_s.at[n], x_r.at[n], up).wait_recv()
    main, rest = pc[0:64, :], pc[64:128, 0:256]
    for n in range(3):
        main = main + r_x[n, :, 0:DS].astype(F32)
        rest = rest + r_x[n, :, DS:WG].astype(F32)
    s_y[:, 0:DS] = main
    s_y[:, DS:WG] = rest
    for n, d in enumerate((2, 1, 3)):
        there = pl.ds(pl.multiple_of(16 * ((yh + d) % NYH), 16), 16)
        s_x[3, 16 * n : 16 * n + 16, :] = s_y[there, :].astype(BF)
        c = remote(s_x.at[3, pl.ds(16 * n, 16), :], r_y.at[n], y_s.at[n], y_r.at[n], ys[d - 1])
        c.start()
        pending.append(c)

    def unfold(acc, out):
        out[0:16, :] = acc[:, 0:DS]
        for q in range(4):
            out[16:20, 256 * q : 256 * q + 256] = acc[4 * q : 4 * q + 4, DS:WG]

    for dy in range(2):
        for dz in range(NZ):
            if (dy, dz) != (0, 0):
                s = at_cap(dy, dz)
                remote(ri.at[s], ri.at[s], ri_s.at[0], ri_r.at[s], up).wait_recv()
    ri[me_i] = si[pl.ds(pl.multiple_of(16 * me_i, 16), 16), :]
    acc = ri[0].astype(F32)
    for n in range(1, NI):
        acc = acc + ri[n].astype(F32)
    unfold(acc, oi_ref)

    acc = s_y[pl.ds(pl.multiple_of(16 * yh, 16), 16), :]
    for n in range(3):
        remote(r_y.at[n], r_y.at[n], y_s.at[n], y_r.at[n], up).wait_recv()
        acc = acc + r_y[n].astype(F32)
    unfold(acc, oc_ref)

    for c in pending:
        c.wait_send()


def local(image_student, caption_student, image_teacher, caption_teacher):
    vmem = pl.BlockSpec(memory_space=pltpu.VMEM)
    dma = pltpu.SemaphoreType.DMA
    out = jax.ShapeDtypeStruct((B, DS), F32)
    return pl.pallas_call(
        kernel,
        out_shape=(out, out),
        in_specs=[vmem] * 4,
        out_specs=(vmem, vmem),
        scratch_shapes=[
            pltpu.VMEM((RI, W), BF),
            pltpu.VMEM((RC, W), BF),
            pltpu.VMEM((MI - RI, DS + DT), BF),
            pltpu.VMEM((MC - RC, DS + DT), BF),
            pltpu.VMEM((16, 512), F32),
            pltpu.VMEM((MI, MC), F32),
            pltpu.VMEM((MI, MC), F32),
            pltpu.VMEM((MI, MC), F32),
            pltpu.VMEM((MI, MC), F32),
            pltpu.VMEM((2, MI, 1), F32),
            pltpu.VMEM((LI, 128), F32),
            pltpu.VMEM((128, LI), F32),
            pltpu.VMEM((NI, 2, LI), F32),
            pltpu.VMEM((NC, 2, MC), F32),
            pltpu.VMEM((MI, MC), BF),
            pltpu.VMEM((MI, DS), F32),
            pltpu.VMEM((RI, WG), BF),
            pltpu.VMEM((NI, 16, WG), BF),
            pltpu.VMEM((MC, DS), F32),
            pltpu.VMEM((RC, WG), F32),
            pltpu.VMEM((4, 64, WG), F32),
            pltpu.VMEM((4, 64, WG), BF),
            pltpu.VMEM((3, 64, WG), BF),
            pltpu.VMEM((64, WG), F32),
            pltpu.VMEM((3, 16, WG), BF),
            dma((NI,)), dma((15,)), dma((NC,)), dma((34,)),
            dma((NI,)), dma((NI,)), dma((NC,)), dma((NC,)),
            dma((NI,)), dma((NI,)), dma((4,)), dma((4,)),
            dma((3,)), dma((3,)), dma((3,)), dma((3,)),
        ],
        compiler_params=pltpu.CompilerParams(
            collective_id=0, has_side_effects=True, vmem_limit_bytes=48 * 2**20
        ),
        cost_estimate=pl.CostEstimate(flops=1_600_000_000, bytes_accessed=400_000, transcendentals=900_000),
        name="contrastive",
    )(image_student, caption_student, image_teacher, caption_teacher)


def solution(mesh):
    return jax.shard_map(
        local,
        mesh=mesh,
        in_specs=(
            P(("img", "cap"), None),
            P(("cap", "img"), None),
            P(("img", "cap"), None),
            P(("cap", "img"), None),
        ),
        out_specs=(P(("img", "cap"), None), P(("cap", "img"), None)),
        check_vma=False,
    )
```

time: 530 us -> 75.5 us (0.14); the launches traced: 521 us -> 75.1 us
  blocking collectives: 460 us -> 0 us
  Pallas kernels: 0 us -> 70 us
  starting transfers between devices: 25 us -> 0 us
  between operations: 15.6 us -> 0.65 us
  local copies, waits for them, and re-layouts: 10.2 us -> 4.41 us
    unnamed x2 -> x0, blocking collectives: 133 us -> none
    all_gather x3 -> x0, blocking collectives: 123 us -> none  [the longest x1 58.1 us: local(): lax.all_gather(caption_teacher, 'img', axis=0, tiled=True)]
    pmax x2 -> x0, blocking collectives: 102 us -> none  [the longest x1 76.9 us: column_pool(): peak_s, peak_t = lax.pmax((parts[0], parts[2]), 'img')]
    psum x2 -> x0, blocking collectives: 102 us -> none  [the longest x1 77.9 us: column_pool(): lax.psum((parts[1] * jnp.exp(parts[0] - peak_s), parts[3] * jnp.exp(parts...]
    pallas_call x0 -> x1, Pallas kernels: none -> 70 us  [local(): pl.pallas_call(kernel, out_shape=(out, out), in_specs=[vmem] * 4, out_spe...]
    unnamed x9 -> x0, starting transfers between devices: 25 us -> none
    unnamed x20 -> x10, local copies, waits for them, and re-layouts: 10.2 us -> 4.41 us
  transfers between devices with their start and end apart: 10 -> 0, of which waited for: 1 -> 0; matrix products, arithmetic and copies ran while one was open for 21% -> 0% of each run, Pallas kernels for 0% -> 0%
where the time goes in v1:
time: 75.5 us; the launch traced here: 75.1 us
  Pallas kernels  70 us (93%)
  local copies, waits for them, and re-layouts  4.41 us (6%)
    pallas_call x1, Pallas kernels, local(): pl.pallas_call(kernel, out_shape=(out, out), in_specs=[vmem] * 4, out_spe...  70 us
    unnamed x10, local copies, waits for them, and re-layouts  4.41 us

profile of v1, /device:TPU:1, one launch (start us, length us, event | category | flops | bytes accessed | tf_op | source)
XLA Modules:
  0.0 75.1 jit_solution(9277653947544590137)
XLA Ops:
  0.6 0.0 copy-start
  0.6 0.8 %copy-done = bf16[20,1024]{1,0:T(8,128)(2,1)S(1)} copy-done((bf16[20,1024]{1,0:T(8,128)(2,1)S(1)}, bf16[20,1024]{1,0:T(8,128)(2,1)}, u32[]{:S(2)}) %copy-start) | copy-done | bytes 40984
  1.4 0.0 copy-start.1
  1.4 0.8 %copy-done.1 = bf16[20,1024]{1,0:T(8,128)(2,1)S(1)} copy-done((bf16[20,1024]{1,0:T(8,128)(2,1)S(1)}, bf16[20,1024]{1,0:T(8,128)(2,1)}, u32[]{:S(2)}) %copy-start.1) | copy-done | bytes 40984
  2.2 0.0 copy-start.2
  2.2 0.8 %copy-done.2 = bf16[20,768]{1,0:T(8,128)(2,1)S(1)} copy-done((bf16[20,768]{1,0:T(8,128)(2,1)S(1)}, bf16[20,768]{1,0:T(8,128)(2,1)}, u32[]{:S(2)}) %copy-start.2) | copy-done | bytes 30744
  3.0 0.0 copy-start.3
  3.0 0.8 %copy-done.3 = bf16[20,768]{1,0:T(8,128)(2,1)S(1)} copy-done((bf16[20,768]{1,0:T(8,128)(2,1)S(1)}, bf16[20,768]{1,0:T(8,128)(2,1)}, u32[]{:S(2)}) %copy-start.3) | copy-done | bytes 30744
  3.8 70.0 %contrastive.1 = (f32[20,1024]{1,0:T(8,128)S(1)}, f32[20,1024]{1,0:T(8,128)S(1)}) custom-call(bf16[20,1024]{1,0:T(8,128)(2,1)S(1)} %copy-done, bf16[20,1024]{1,0:T(8,128)(2,1)S(1)} %copy-done.1, bf16[20,768]{1,0:T(8,128)(2,1)S(1)} %copy-done.2, bf16[20,768]{1,0:T(8,128)(2,1)S(1)} %copy-done.3), custom_call_target="tpu_custom_call" | custom-call | flops 1600000000 | bytes 400000 | tf_op jit(solution)/shard_map/contrastive/pallas_call | solution.py:403
  73.8 0.6 copy.8
  74.5 0.6 copy.9
Async XLA Ops:
  0.6 0.8 %copy-start = (bf16[20,1024]{1,0:T(8,128)(2,1)S(1)}, bf16[20,1024]{1,0:T(8,128)(2,1)}, u32[]{:S(2)}) copy-start(bf16[20,1024]{1,0:T(8,128)(2,1)} %is_ref.1) | copy-start | bytes 122884
  1.4 0.8 %copy-start.1 = (bf16[20,1024]{1,0:T(8,128)(2,1)S(1)}, bf16[20,1024]{1,0:T(8,128)(2,1)}, u32[]{:S(2)}) copy-start(bf16[20,1024]{1,0:T(8,128)(2,1)} %cs_ref.1) | copy-start | bytes 122884
  2.2 0.8 %copy-start.2 = (bf16[20,768]{1,0:T(8,128)(2,1)S(1)}, bf16[20,768]{1,0:T(8,128)(2,1)}, u32[]{:S(2)}) copy-start(bf16[20,768]{1,0:T(8,128)(2,1)} %it_ref.1) | copy-start | bytes 92164
  3.0 0.8 %copy-start.3 = (bf16[20,768]{1,0:T(8,128)(2,1)S(1)}, bf16[20,768]{1,0:T(8,128)(2,1)}, u32[]{:S(2)}) copy-start(bf16[20,768]{1,0:T(8,128)(2,1)} %ct_ref.1) | copy-start | bytes 92164

commit v2 on v1

--- a/solution.py
+++ b/solution.py
@@ -37,11 +37,12 @@
 
 
 def kernel(
-    is_ref, cs_ref, it_ref, ct_ref, oi_ref, oc_ref,
-    gi, gc, ar, br, rp, es, et, fs, ft, rmx, tb, tb2, rxr, rxc,
-    tg, pi, si, ri, pc, sc, r_core, s_x, r_x, s_y, r_y,
-    gi_r, gi_s, gc_r, gc_s, lr_r, lr_s, lc_r, lc_s,
-    ri_r, ri_s, co_r, co_s, x_r, x_s, y_r, y_s,
+    is_hbm, cs_hbm, it_hbm, ct_hbm, oi_ref, oc_ref,
+    is_ref, cs_ref, it_ref, ct_ref,
+    gi, gc, ar, br, rp, es, et, fs, ft, rmx, tb, tb2, rxr, rxc, rxr2, rxc2,
+    tg, pi, si, s_p, r_p, s_z, r_z, pc, sc, r_core, s_x, r_x, s_y, r_y,
+    in_sem, gi_r, gi_s, gc_r, gc_s, lr_r, lr_s, lc_r, lc_s, mr_r, mr_s, mc_r, mc_s,
+    p_r, p_s, z_r, z_s, co_r, co_s, x_r, x_s, y_r, y_s,
 ):
     img, cap = lax.axis_index("img"), lax.axis_index("cap")
     yh, x, core = img // (2 * NX), (img // 2) % NX, img % 2
@@ -70,6 +71,14 @@
     near = [up, down, pair, xu, xd, x2, sib] + ys
     for dev in near:
         pl.semaphore_signal(barrier, inc=1, device_id=dev, device_id_type=MESH)
+
+    loads = []
+    for n, (src, dst) in enumerate(((is_hbm, is_ref), (cs_hbm, cs_ref), (it_hbm, it_ref), (ct_hbm, ct_ref))):
+        c = pltpu.make_async_copy(src, dst, in_sem.at[n])
+        c.start()
+        loads.append(c)
+    for c in loads:
+        c.wait()
 
     me_i, me_c = cap, slot_c(0, 0, 0)
     for s_ref, t_ref, buf, slot in ((is_ref, it_ref, gi, me_i), (cs_ref, ct_ref, gc, me_c)):
@@ -181,26 +190,26 @@
     cap_y(3)
     img_pair_up(1)
     img_pair_down(1)
-    cap_y(2)
+    cap_x2(0)
     img_own_up(2)
     img_own_down(2)
     cap_xu(1)
+    cap_xd(1)
+    cap_y(2)
+    img_pair_up(2)
+    cap_xu(3)
     cap_xd(3)
-    cap_x2(0)
-    img_pair_up(2)
     img_pair_down(2)
-    cap_xu(3)
-    cap_xd(1)
     img_own_up(3)
     img_own_down(3)
+    cap_x2(1)
+    cap_xd(2)
     cap_xu(2)
-    cap_xd(2)
     img_pair_up(3)
     img_pair_down(3)
     cap_x2(3)
-    cap_x2(1)
+    img_own_up(4)
     cap_x2(2)
-    img_own_up(4)
     img_pair_down(4)
     for dx in range(NX):
         for j in range(NYH):
@@ -248,45 +257,48 @@
     for n, b in enumerate(range(0, MI, 64)):
         tb[b : b + 64, :] = jnp.where(lane == 0, row_lse[0][n], jnp.where(lane == 1, row_lse[1][n], 0.0))
     tb[MI:LI, :] = jnp.zeros((LI - MI, 128), F32)
-    rxr[me_i] = tb[...].T[0:2, :]
-    rxc[me_c, 0:1, :] = col_lse[0]
-    rxc[me_c, 1:2, :] = col_lse[1]
-
-    for j in range(NYH):
-        for dx in range(NX):
-            for dc in range(2):
-                if (j, dx, dc) != (0, 0, 0):
-                    n = (j * NX + dx) * 2 + dc
-                    c = remote(rxc.at[me_c], rxc.at[me_c], lc_s.at[n], lc_r.at[me_c], (at_img(j, dx, dc), cap))
-                    c.start()
-                    pending.append(c)
-    for dy in range(2):
-        for dz in range(NZ):
-            if (dy, dz) != (0, 0):
-                n = dy * NZ + dz
-                c = remote(rxr.at[me_i], rxr.at[me_i], lr_s.at[n], lr_r.at[me_i], (img, at_cap(dy, dz)))
-                c.start()
-                pending.append(c)
-    for dy in range(2):
-        for dz in range(NZ):
-            if (dy, dz) != (0, 0):
-                s = at_cap(dy, dz)
-                remote(rxr.at[s], rxr.at[s], lr_s.at[0], lr_r.at[s], up).wait_recv()
-    for j in range(NYH):
-        for dx in range(NX):
-            for dc in range(2):
-                if (j, dx, dc) != (0, 0, 0):
-                    s = slot_c(j, dx, dc)
-                    remote(rxc.at[s], rxc.at[s], lc_s.at[0], lc_r.at[s], up).wait_recv()
+    me_x = x * 2 + core
+    rxc[me_x, 0:1, :] = col_lse[0]
+    rxc[me_x, 1:2, :] = col_lse[1]
+    peers_x = [(dx, dc) for dx in (2, 1, 3, 0) for dc in (1, 0) if (dx, dc) != (0, 0)]
+    for n, (dx, dc) in enumerate(peers_x):
+        c = remote(rxc.at[me_x], rxc.at[me_x], lc_s.at[n], lc_r.at[me_x], (at_img(0, dx, dc), cap))
+        c.start()
+        pending.append(c)
+    rxr[z] = tb[...].T[0:2, :]
+    peers_z = (4, 3, 5, 2, 6, 1, 7)
+    for n, dz in enumerate(peers_z):
+        c = remote(rxr.at[z], rxr.at[z], lr_s.at[n], lr_r.at[z], (img, at_cap(0, dz)))
+        c.start()
+        pending.append(c)
 
     def pool(parts):
         m = jnp.max(parts, axis=0)
         return m + jnp.log(jnp.sum(jnp.exp(parts - m[None]), axis=0))
 
     tb2[...] = jnp.zeros_like(tb2)
-    tb2[0:2, :] = pool(rxr[...])
+    for dx, dc in reversed(peers_x):
+        s = ((x + dx) % NX) * 2 + (core + dc) % 2
+        remote(rxc.at[s], rxc.at[s], lc_s.at[0], lc_r.at[s], up).wait_recv()
+    rxc2[yh] = pool(rxc[...])
+    for n, d in enumerate((2, 1, 3)):
+        c = remote(rxc2.at[yh], rxc2.at[yh], mc_s.at[n], mc_r.at[yh], ys[d - 1])
+        c.start()
+        pending.append(c)
+    for dz in reversed(peers_z):
+        s = (z + dz) % NZ
+        remote(rxr.at[s], rxr.at[s], lr_s.at[0], lr_r.at[s], up).wait_recv()
+    rxr2[yl] = pool(rxr[...])
+    c = remote(rxr2.at[yl], rxr2.at[yl], mr_s.at[0], mr_r.at[yl], pair)
+    c.start()
+    pending.append(c)
+    remote(rxr2.at[1 - yl], rxr2.at[1 - yl], mr_s.at[0], mr_r.at[1 - yl], up).wait_recv()
+    tb2[0:2, :] = pool(rxr2[...])
     rows_all = tb2[...].T
-    cols_all = pool(rxc[...])
+    for d in (1, 3, 2):
+        s = (yh + d) % NYH
+        remote(rxc2.at[s], rxc2.at[s], mc_s.at[0], mc_r.at[s], up).wait_recv()
+    cols_all = pool(rxc2[...])
     f_col_s = 0.5 * jnp.exp(col_max[0] - cols_all[0:1, :])
     f_col_t = 0.25 * jnp.exp(col_max[1] - cols_all[1:2, :])
 
@@ -309,14 +321,32 @@
         g = g - jnp.where(row_id == col_id, 0.5, 0.0)
         tg[rows, :] = g.astype(BF)
 
+    def folded(v):
+        v = jnp.concatenate([v[:, 256 * q : 256 * q + 256] for q in range(4)], axis=0)
+        hi = v.astype(BF)
+        lo = (v - hi.astype(F32)).astype(BF)
+        return t_dot(fold, hi) + t_dot(fold, lo)
+
+    pi[...] = jnp.dot(tg[:, 0:RC], gc[:, 0:DS], preferred_element_type=F32) + jnp.dot(
+        tg[:, RC:MC], br[:, 0:DS], preferred_element_type=F32
+    )
+    si[:, 0:DS] = pi[0:RI, :]
+    si[:, DS:WG] = folded(pi[RI:MI, :])
+    far = (4, 3, 5, 2, 6, 1, 7, 0)
+    pair_copies = []
+    for n, dz in enumerate(far):
+        there = pl.ds(pl.multiple_of(16 * at_cap(1, dz), 16), 16)
+        s_p[n] = si[there, :].astype(BF)
+        c = remote(s_p.at[n], r_p.at[n], p_s.at[n], p_r.at[n], pair)
+        c.start()
+        pair_copies.append(c)
+        pending.append(c)
+
     pc[...] = t_dot(tg[0:RI, :], gi[:, 0:DS]) + t_dot(tg[RI:MI, :], ar[:, 0:DS])
     for h in range(2):
         rows = slice(256 * h, 256 * h + 256)
         sc[rows, 0:DS] = pc[rows, :]
-        rem = jnp.concatenate(
-            [pc[RC + 64 * h : RC + 64 * h + 64, 256 * q : 256 * q + 256] for q in range(4)], axis=0
-        ).astype(BF)
-        sc[rows, DS:WG] = t_dot(fold, rem)
+        sc[rows, DS:WG] = folded(pc[RC + 64 * h : RC + 64 * h + 64, :])
     half = NX * NYH * 16
     core_copies = []
     for n, dx in enumerate((2, 1, 3, 0)):
@@ -326,43 +356,48 @@
         core_copies.append(c)
         pending.append(c)
 
-    pi[...] = jnp.dot(tg[:, 0:RC], gc[:, 0:DS], preferred_element_type=F32) + jnp.dot(
-        tg[:, RC:MC], br[:, 0:DS], preferred_element_type=F32
-    )
-    si[:, 0:DS] = pi[0:RI, :].astype(BF)
-    rem = jnp.concatenate([pi[RI:MI, 256 * q : 256 * q + 256] for q in range(4)], axis=0).astype(BF)
-    si[:, DS:WG] = t_dot(fold, rem).astype(BF)
-    for dz in (4, 3, 5, 2, 6, 1, 7, 0):
-        for dy in range(2):
-            if (dy, dz) != (0, 0):
-                n = dy * NZ + dz
-                s = at_cap(dy, dz)
-                block = si.at[pl.ds(pl.multiple_of(16 * s, 16), 16), :]
-                c = remote(block, ri.at[me_i], ri_s.at[n], ri_r.at[me_i], (img, s))
-                c.start()
-                pending.append(c)
-
-    for n, dx in enumerate((2, 1, 3, 0)):
-        here = pl.ds(pl.multiple_of(core * half + ((x + dx) % NX) * (NYH * 16), 64), 64)
+    def along_z(n):
+        dz = far[n]
+        here = pl.ds(pl.multiple_of(16 * at_cap(0, dz), 16), 16)
+        pair_copies[n].wait_recv()
+        v = si[here, :] + r_p[n].astype(F32)
+        if dz:
+            s_z[n] = v.astype(BF)
+            c = remote(s_z.at[n], r_z.at[n], z_s.at[n], z_r.at[n], (img, at_cap(0, dz)))
+            c.start()
+            pending.append(c)
+        return v
+
+    def along_x(n):
+        here = pl.ds(pl.multiple_of(core * half + ((x + (2, 1, 3, 0)[n]) % NX) * (NYH * 16), 64), 64)
         core_copies[n].wait_recv()
         v = sc[here, :] + r_core[n]
-        if dx:
+        if n < 3:
             s_x[n] = v.astype(BF)
-            dev = (x2, xu, xd)[n]
-            c = remote(s_x.at[n], r_x.at[n], x_s.at[n], x_r.at[n], dev)
+            c = remote(s_x.at[n], r_x.at[n], x_s.at[n], x_r.at[n], (x2, xu, xd)[n])
             c.start()
             pending.append(c)
         else:
-            pc[0:64, :] = v[:, 0:DS]
-            pc[64:128, 0:256] = v[:, DS:WG]
-    for n in range(3):
+            s_y[...] = v
+
+    along_z(0)
+    along_z(1)
+    along_x(0)
+    along_z(2)
+    along_x(1)
+    along_z(3)
+    along_x(2)
+    along_z(4)
+    along_z(5)
+    along_z(6)
+    along_x(3)
+    own_i = along_z(7)
+
+    v = s_y[...]
+    for n in (1, 2, 0):
         remote(r_x.at[n], r_x.at[n], x_s.at[n], x_r.at[n], up).wait_recv()
-    main, rest = pc[0:64, :], pc[64:128, 0:256]
-    for n in range(3):
-        main = main + r_x[n, :, 0:DS].astype(F32)
-        rest = rest + r_x[n, :, DS:WG].astype(F32)
-    s_y[:, 0:DS] = main
-    s_y[:, DS:WG] = rest
+        v = v + r_x[n].astype(F32)
+    s_y[...] = v
     for n, d in enumerate((2, 1, 3)):
         there = pl.ds(pl.multiple_of(16 * ((yh + d) % NYH), 16), 16)
         s_x[3, 16 * n : 16 * n + 16, :] = s_y[there, :].astype(BF)
@@ -375,15 +410,10 @@
         for q in range(4):
             out[16:20, 256 * q : 256 * q + 256] = acc[4 * q : 4 * q + 4, DS:WG]
 
-    for dy in range(2):
-        for dz in range(NZ):
-            if (dy, dz) != (0, 0):
-                s = at_cap(dy, dz)
-                remote(ri.at[s], ri.at[s], ri_s.at[0], ri_r.at[s], up).wait_recv()
-    ri[me_i] = si[pl.ds(pl.multiple_of(16 * me_i, 16), 16), :]
-    acc = ri[0].astype(F32)
-    for n in range(1, NI):
-        acc = acc + ri[n].astype(F32)
+    acc = own_i
+    for n in reversed(range(NZ - 1)):
+        remote(r_z.at[n], r_z.at[n], z_s.at[n], z_r.at[n], up).wait_recv()
+        acc = acc + r_z[n].astype(F32)
     unfold(acc, oi_ref)
 
     acc = s_y[pl.ds(pl.multiple_of(16 * yh, 16), 16), :]
@@ -403,9 +433,13 @@
     return pl.pallas_call(
         kernel,
         out_shape=(out, out),
-        in_specs=[vmem] * 4,
+        in_specs=[pl.BlockSpec(memory_space=pltpu.HBM)] * 4,
         out_specs=(vmem, vmem),
         scratch_shapes=[
+            pltpu.VMEM((B, DS), BF),
+            pltpu.VMEM((B, DS), BF),
+            pltpu.VMEM((B, DT), BF),
+            pltpu.VMEM((B, DT), BF),
             pltpu.VMEM((RI, W), BF),
             pltpu.VMEM((RC, W), BF),
             pltpu.VMEM((MI - RI, DS + DT), BF),
@@ -418,12 +452,17 @@
             pltpu.VMEM((2, MI, 1), F32),
             pltpu.VMEM((LI, 128), F32),
             pltpu.VMEM((128, LI), F32),
-            pltpu.VMEM((NI, 2, LI), F32),
-            pltpu.VMEM((NC, 2, MC), F32),
+            pltpu.VMEM((NZ, 2, LI), F32),
+            pltpu.VMEM((2 * NX, 2, MC), F32),
+            pltpu.VMEM((2, 2, LI), F32),
+            pltpu.VMEM((NYH, 2, MC), F32),
             pltpu.VMEM((MI, MC), BF),
             pltpu.VMEM((MI, DS), F32),
-            pltpu.VMEM((RI, WG), BF),
-            pltpu.VMEM((NI, 16, WG), BF),
+            pltpu.VMEM((RI, WG), F32),
+            pltpu.VMEM((NZ, 16, WG), BF),
+            pltpu.VMEM((NZ, 16, WG), BF),
+            pltpu.VMEM((NZ - 1, 16, WG), BF),
+            pltpu.VMEM((NZ - 1, 16, WG), BF),
             pltpu.VMEM((MC, DS), F32),
             pltpu.VMEM((RC, WG), F32),
             pltpu.VMEM((4, 64, WG), F32),
@@ -431,13 +470,15 @@
             pltpu.VMEM((3, 64, WG), BF),
             pltpu.VMEM((64, WG), F32),
             pltpu.VMEM((3, 16, WG), BF),
-            dma((NI,)), dma((15,)), dma((NC,)), dma((34,)),
-            dma((NI,)), dma((NI,)), dma((NC,)), dma((NC,)),
-            dma((NI,)), dma((NI,)), dma((4,)), dma((4,)),
-            dma((3,)), dma((3,)), dma((3,)), dma((3,)),
+            dma((4,)),
+            dma((NI,)), dma((15,)), dma((NC,)), dma((31,)),
+            dma((8,)), dma((7,)), dma((8,)), dma((7,)),
+            dma((2,)), dma((1,)), dma((4,)), dma((3,)),
+            dma((8,)), dma((8,)), dma((7,)), dma((7,)),
+            dma((4,)), dma((4,)), dma((3,)), dma((3,)), dma((3,)), dma((3,)),
         ],
         compiler_params=pltpu.CompilerParams(
-            collective_id=0, has_side_effects=True, vmem_limit_bytes=48 * 2**20
+            collective_id=0, has_side_effects=True, vmem_limit_bytes=63 * 2**20
         ),
         cost_estimate=pl.CostEstimate(flops=1_600_000_000, bytes_accessed=400_000, transcendentals=900_000),
         name="contrastive",

time: 75.5 us -> 71.5 us (0.947)
  local copies, waits for them, and re-layouts: 4.41 us -> 2.22 us
  Pallas kernels: 70 us -> 68.5 us
    unnamed x10 -> x4, local copies, waits for them, and re-layouts: 4.41 us -> 2.22 us
    pallas_call x1, Pallas kernels: 70 us -> 68.5 us  [local(): pl.pallas_call(kernel, out_shape=(out, out), in_specs=[pl.BlockSpec(memor...]
where the time goes in v2:
time: 71.5 us; the launch traced here: 71.3 us
  Pallas kernels  68.5 us (96%)
  local copies, waits for them, and re-layouts  2.22 us (3%)
    pallas_call x1, Pallas kernels, local(): pl.pallas_call(kernel, out_shape=(out, out), in_specs=[pl.BlockSpec(memor...  68.5 us
    unnamed x4, local copies, waits for them, and re-layouts  2.22 us

profile of v2, /device:TPU:1, one launch (start us, length us, event | category | flops | bytes accessed | tf_op | source)
XLA Modules:
  0.0 71.3 jit_solution(15499938297179973592)
XLA Ops:
  0.6 68.5 %contrastive.1 = (f32[20,1024]{1,0:T(8,128)}, f32[20,1024]{1,0:T(8,128)}) custom-call(bf16[20,1024]{1,0:T(8,128)(2,1)} %is_hbm.1, bf16[20,1024]{1,0:T(8,128)(2,1)} %cs_hbm.1, bf16[20,768]{1,0:T(8,128)(2,1)} %it_hbm.1, bf16[20,768]{1,0:T(8,128)(2,1)} %ct_hbm.1), custom_call_target="tpu_custom_call" | custom-call | flops 1600000000 | bytes 400000 | tf_op jit(solution)/shard_map/contrastive/pallas_call | solution.py:433
  69.1 0.0 copy-start
  69.1 1.6 %copy.8 = f32[20,1024]{1,0:T(8,128)} copy(f32[20,1024]{1,0:T(8,128)} %get-tuple-element.4) | data formatting | bytes 163840
  70.7 0.0 copy-done
  70.7 0.6 copy.9
Async XLA Ops:
  69.1 1.6 %copy-start = (f32[20,1024]{1,0:T(8,128)S(1)}, f32[20,1024]{1,0:T(8,128)}, u32[]{:S(2)}) copy-start(f32[20,1024]{1,0:T(8,128)} %get-tuple-element.5) | copy-start | bytes 245764

commit v3 on v2

--- a/solution.py
+++ b/solution.py
@@ -39,9 +39,9 @@
 def kernel(
     is_hbm, cs_hbm, it_hbm, ct_hbm, oi_ref, oc_ref,
     is_ref, cs_ref, it_ref, ct_ref,
-    gi, gc, ar, br, rp, es, et, fs, ft, rmx, tb, tb2, rxr, rxc, rxr2, rxc2,
-    tg, pi, si, s_p, r_p, s_z, r_z, pc, sc, r_core, s_x, r_x, s_y, r_y,
-    in_sem, gi_r, gi_s, gc_r, gc_s, lr_r, lr_s, lc_r, lc_s, mr_r, mr_s, mc_r, mc_s,
+    gi, gc, ar, br, rp, es, et, fs, ft, rmx, tb, tb2, rxr, rxk, rxc,
+    tg, pi, si, s_p, r_p, s_z, r_z, pc, sc, r_core, s_v, s_x, r_x, s_y, r_y,
+    in_sem, gi_r, gi_s, gc_r, gc_s, lr_r, lr_s, lk_r, lk_s, lc_r, lc_s,
     p_r, p_s, z_r, z_s, co_r, co_s, x_r, x_s, y_r, y_s,
 ):
     img, cap = lax.axis_index("img"), lax.axis_index("cap")
@@ -52,7 +52,7 @@
         return (((yh + dyh) % NYH) * NX + (x + dx) % NX) * 2 + (core + dcore) % 2
 
     def slot_c(dyh, dx, dcore):
-        return ((core + dcore) % 2) * (NX * NYH) + ((x + dx) % NX) * NYH + (yh + dyh) % NYH
+        return ((core + dcore) % 2) * (NX * NYH) + ((yh + dyh) % NYH) * NX + (x + dx) % NX
 
     def at_cap(dyl, dz):
         return ((yl + dyl) % 2) * NZ + (z + dz) % NZ
@@ -257,18 +257,15 @@
     for n, b in enumerate(range(0, MI, 64)):
         tb[b : b + 64, :] = jnp.where(lane == 0, row_lse[0][n], jnp.where(lane == 1, row_lse[1][n], 0.0))
     tb[MI:LI, :] = jnp.zeros((LI - MI, 128), F32)
-    me_x = x * 2 + core
-    rxc[me_x, 0:1, :] = col_lse[0]
-    rxc[me_x, 1:2, :] = col_lse[1]
-    peers_x = [(dx, dc) for dx in (2, 1, 3, 0) for dc in (1, 0) if (dx, dc) != (0, 0)]
-    for n, (dx, dc) in enumerate(peers_x):
-        c = remote(rxc.at[me_x], rxc.at[me_x], lc_s.at[n], lc_r.at[me_x], (at_img(0, dx, dc), cap))
-        c.start()
-        pending.append(c)
-    rxr[z] = tb[...].T[0:2, :]
-    peers_z = (4, 3, 5, 2, 6, 1, 7)
-    for n, dz in enumerate(peers_z):
-        c = remote(rxr.at[z], rxr.at[z], lr_s.at[n], lr_r.at[z], (img, at_cap(0, dz)))
+    rxk[core, 0:1, :] = col_lse[0]
+    rxk[core, 1:2, :] = col_lse[1]
+    c = remote(rxk.at[core], rxk.at[core], lk_s.at[0], lk_r.at[core], sib)
+    c.start()
+    pending.append(c)
+    rxr[me_i] = tb[...].T[0:2, :]
+    peers_r = [(dy, dz) for dz in (4, 3, 5, 2, 6, 1, 7, 0) for dy in (1, 0) if (dy, dz) != (0, 0)]
+    for n, (dy, dz) in enumerate(peers_r):
+        c = remote(rxr.at[me_i], rxr.at[me_i], lr_s.at[n], lr_r.at[me_i], (img, at_cap(dy, dz)))
         c.start()
         pending.append(c)
 
@@ -277,35 +274,30 @@
         return m + jnp.log(jnp.sum(jnp.exp(parts - m[None]), axis=0))
 
     tb2[...] = jnp.zeros_like(tb2)
-    for dx, dc in reversed(peers_x):
-        s = ((x + dx) % NX) * 2 + (core + dc) % 2
-        remote(rxc.at[s], rxc.at[s], lc_s.at[0], lc_r.at[s], up).wait_recv()
-    rxc2[yh] = pool(rxc[...])
-    for n, d in enumerate((2, 1, 3)):
-        c = remote(rxc2.at[yh], rxc2.at[yh], mc_s.at[n], mc_r.at[yh], ys[d - 1])
+    remote(rxk.at[1 - core], rxk.at[1 - core], lk_s.at[0], lk_r.at[1 - core], up).wait_recv()
+    me_x = yh * NX + x
+    rxc[me_x] = pool(rxk[...])
+    peers_c = [(j, dx) for j in (2, 1, 3, 0) for dx in (2, 1, 3, 0) if (j, dx) != (0, 0)]
+    for n, (j, dx) in enumerate(peers_c):
+        c = remote(rxc.at[me_x], rxc.at[me_x], lc_s.at[n], lc_r.at[me_x], (at_img(j, dx, 0), cap))
         c.start()
         pending.append(c)
-    for dz in reversed(peers_z):
-        s = (z + dz) % NZ
+    for dy, dz in reversed(peers_r):
+        s = at_cap(dy, dz)
         remote(rxr.at[s], rxr.at[s], lr_s.at[0], lr_r.at[s], up).wait_recv()
-    rxr2[yl] = pool(rxr[...])
-    c = remote(rxr2.at[yl], rxr2.at[yl], mr_s.at[0], mr_r.at[yl], pair)
-    c.start()
-    pending.append(c)
-    remote(rxr2.at[1 - yl], rxr2.at[1 - yl], mr_s.at[0], mr_r.at[1 - yl], up).wait_recv()
-    tb2[0:2, :] = pool(rxr2[...])
+    tb2[0:2, :] = pool(rxr[...])
     rows_all = tb2[...].T
-    for d in (1, 3, 2):
-        s = (yh + d) % NYH
-        remote(rxc2.at[s], rxc2.at[s], mc_s.at[0], mc_r.at[s], up).wait_recv()
-    cols_all = pool(rxc2[...])
+    for j, dx in reversed(peers_c):
+        s = ((yh + j) % NYH) * NX + (x + dx) % NX
+        remote(rxc.at[s], rxc.at[s], lc_s.at[0], lc_r.at[s], up).wait_recv()
+    cols_all = pool(rxc[...])
     f_col_s = 0.5 * jnp.exp(col_max[0] - cols_all[0:1, :])
     f_col_t = 0.25 * jnp.exp(col_max[1] - cols_all[1:2, :])
 
     b = lax.broadcasted_iota(jnp.int32, (1, MC), 1)
     t = jnp.where(b < RC, b >> 4, (b - RC) >> 2)
     u = jnp.where(b < RC, b & 15, 16 + (b & 3))
-    block = (t & 3) * (2 * NX) + ((t >> 2) & 3) * 2 + (t >> 4)
+    block = (t >> 2 & 3) * (2 * NX) + (t & 3) * 2 + (t >> 4)
     col_id = cap * MC + block * B + u
     for lo in range(0, MI, 64):
         a = lo + lax.broadcasted_iota(jnp.int32, (64, 1), 0)
@@ -327,6 +319,25 @@
         lo = (v - hi.astype(F32)).astype(BF)
         return t_dot(fold, hi) + t_dot(fold, lo)
 
+    pc[...] = t_dot(tg[0:RI, :], gi[:, 0:DS]) + t_dot(tg[RI:MI, :], ar[:, 0:DS])
+    for h in range(2):
+        rows = slice(256 * h, 256 * h + 256)
+        sc[rows, 0:DS] = pc[rows, :]
+        sc[rows, DS:WG] = folded(pc[RC + 64 * h : RC + 64 * h + 64, :])
+    group = NX * 16
+
+    def group_at(dcore, d):
+        at = ((core + dcore) % 2) * NYH + (yh + d) % NYH
+        return pl.ds(pl.multiple_of(group * at, group), group)
+
+    order_y = (2, 1, 3, 0)
+    core_copies = []
+    for n, d in enumerate(order_y):
+        c = remote(sc.at[group_at(1, d), :], r_core.at[n], co_s.at[n], co_r.at[n], sib)
+        c.start()
+        core_copies.append(c)
+        pending.append(c)
+
     pi[...] = jnp.dot(tg[:, 0:RC], gc[:, 0:DS], preferred_element_type=F32) + jnp.dot(
         tg[:, RC:MC], br[:, 0:DS], preferred_element_type=F32
     )
@@ -342,20 +353,6 @@
         pair_copies.append(c)
         pending.append(c)
 
-    pc[...] = t_dot(tg[0:RI, :], gi[:, 0:DS]) + t_dot(tg[RI:MI, :], ar[:, 0:DS])
-    for h in range(2):
-        rows = slice(256 * h, 256 * h + 256)
-        sc[rows, 0:DS] = pc[rows, :]
-        sc[rows, DS:WG] = folded(pc[RC + 64 * h : RC + 64 * h + 64, :])
-    half = NX * NYH * 16
-    core_copies = []
-    for n, dx in enumerate((2, 1, 3, 0)):
-        there = pl.ds(pl.multiple_of((1 - core) * half + ((x + dx) % NX) * (NYH * 16), 64), 64)
-        c = remote(sc.at[there, :], r_core.at[n], co_s.at[n], co_r.at[n], sib)
-        c.start()
-        core_copies.append(c)
-        pending.append(c)
-
     def along_z(n):
         dz = far[n]
         here = pl.ds(pl.multiple_of(16 * at_cap(0, dz), 16), 16)
@@ -369,41 +366,46 @@
         return v
 
     def along_x(n):
-        here = pl.ds(pl.multiple_of(core * half + ((x + (2, 1, 3, 0)[n]) % NX) * (NYH * 16), 64), 64)
         core_copies[n].wait_recv()
-        v = sc[here, :] + r_core[n]
-        if n < 3:
-            s_x[n] = v.astype(BF)
-            c = remote(s_x.at[n], r_x.at[n], x_s.at[n], x_r.at[n], (x2, xu, xd)[n])
+        v = sc[group_at(0, order_y[n]), :] + r_core[n]
+        s_v[n] = v
+        s_x[n] = v.astype(BF)
+        for k, (dx, dev) in enumerate(((2, x2), (1, xu), (3, xd))):
+            there = pl.ds(pl.multiple_of(16 * ((x + dx) % NX), 16), 16)
+            m = 3 * n + k
+            c = remote(s_x.at[n, there, :], r_x.at[m], x_s.at[m], x_r.at[m], dev)
             c.start()
             pending.append(c)
-        else:
-            s_y[...] = v
-
+
+    def along_y(n):
+        v = s_v[n, pl.ds(pl.multiple_of(16 * x, 16), 16), :]
+        for k in (1, 2, 0):
+            m = 3 * n + k
+            remote(r_x.at[m], r_x.at[m], x_s.at[m], x_r.at[m], up).wait_recv()
+            v = v + r_x[m].astype(F32)
+        if n < 3:
+            s_y[n] = v.astype(BF)
+            c = remote(s_y.at[n], r_y.at[n], y_s.at[n], y_r.at[n], ys[order_y[n] - 1])
+            c.start()
+            pending.append(c)
+        return v
+
+    along_x(0)
+    along_x(1)
     along_z(0)
+    along_x(2)
     along_z(1)
-    along_x(0)
+    along_x(3)
     along_z(2)
-    along_x(1)
+    along_y(0)
     along_z(3)
-    along_x(2)
+    along_y(1)
     along_z(4)
     along_z(5)
+    along_y(2)
     along_z(6)
-    along_x(3)
     own_i = along_z(7)
-
-    v = s_y[...]
-    for n in (1, 2, 0):
-        remote(r_x.at[n], r_x.at[n], x_s.at[n], x_r.at[n], up).wait_recv()
-        v = v + r_x[n].astype(F32)
-    s_y[...] = v
-    for n, d in enumerate((2, 1, 3)):
-        there = pl.ds(pl.multiple_of(16 * ((yh + d) % NYH), 16), 16)
-        s_x[3, 16 * n : 16 * n + 16, :] = s_y[there, :].astype(BF)
-        c = remote(s_x.at[3, pl.ds(16 * n, 16), :], r_y.at[n], y_s.at[n], y_r.at[n], ys[d - 1])
-        c.start()
-        pending.append(c)
+    own_c = along_y(3)
 
     def unfold(acc, out):
         out[0:16, :] = acc[:, 0:DS]
@@ -416,8 +418,8 @@
         acc = acc + r_z[n].astype(F32)
     unfold(acc, oi_ref)
 
-    acc = s_y[pl.ds(pl.multiple_of(16 * yh, 16), 16), :]
-    for n in range(3):
+    acc = own_c
+    for n in (1, 2, 0):
         remote(r_y.at[n], r_y.at[n], y_s.at[n], y_r.at[n], up).wait_recv()
         acc = acc + r_y[n].astype(F32)
     unfold(acc, oc_ref)
@@ -429,7 +431,7 @@
 def local(image_student, caption_student, image_teacher, caption_teacher):
     vmem = pl.BlockSpec(memory_space=pltpu.VMEM)
     dma = pltpu.SemaphoreType.DMA
-    out = jax.ShapeDtypeStruct((B, DS), F32)
+    out = pltpu.VMEM((B, DS), F32)
     return pl.pallas_call(
         kernel,
         out_shape=(out, out),
@@ -452,10 +454,9 @@
             pltpu.VMEM((2, MI, 1), F32),
             pltpu.VMEM((LI, 128), F32),
             pltpu.VMEM((128, LI), F32),
-            pltpu.VMEM((NZ, 2, LI), F32),
-            pltpu.VMEM((2 * NX, 2, MC), F32),
-            pltpu.VMEM((2, 2, LI), F32),
-            pltpu.VMEM((NYH, 2, MC), F32),
+            pltpu.VMEM((NI, 2, LI), F32),
+            pltpu.VMEM((2, 2, MC), F32),
+            pltpu.VMEM((NX * NYH, 2, MC), F32),
             pltpu.VMEM((MI, MC), BF),
             pltpu.VMEM((MI, DS), F32),
             pltpu.VMEM((RI, WG), F32),
@@ -466,23 +467,23 @@
             pltpu.VMEM((MC, DS), F32),
             pltpu.VMEM((RC, WG), F32),
             pltpu.VMEM((4, 64, WG), F32),
+            pltpu.VMEM((4, 64, WG), F32),
             pltpu.VMEM((4, 64, WG), BF),
-            pltpu.VMEM((3, 64, WG), BF),
-            pltpu.VMEM((64, WG), F32),
+            pltpu.VMEM((12, 16, WG), BF),
+            pltpu.VMEM((3, 16, WG), BF),
             pltpu.VMEM((3, 16, WG), BF),
             dma((4,)),
             dma((NI,)), dma((15,)), dma((NC,)), dma((31,)),
-            dma((8,)), dma((7,)), dma((8,)), dma((7,)),
-            dma((2,)), dma((1,)), dma((4,)), dma((3,)),
+            dma((NI,)), dma((15,)), dma((2,)), dma((1,)), dma((16,)), dma((15,)),
             dma((8,)), dma((8,)), dma((7,)), dma((7,)),
-            dma((4,)), dma((4,)), dma((3,)), dma((3,)), dma((3,)), dma((3,)),
+            dma((4,)), dma((4,)), dma((12,)), dma((12,)), dma((3,)), dma((3,)),
         ],
         compiler_params=pltpu.CompilerParams(
-            collective_id=0, has_side_effects=True, vmem_limit_bytes=63 * 2**20
+            collective_id=0, has_side_effects=True, vmem_limit_bytes=56 * 2**20
         ),
         cost_estimate=pl.CostEstimate(flops=1_600_000_000, bytes_accessed=400_000, transcendentals=900_000),
         name="contrastive",
-    )(image_student, caption_student, image_teacher, caption_teacher)
+    )(*(pltpu.with_memory_space_constraint(a, pltpu.HBM) for a in (image_student, caption_student, image_teacher, caption_teacher)))
 
 
 def solution(mesh):

time: 71.5 us -> 65.2 us (0.912); the launches traced: 71.3 us -> 63.9 us
  Pallas kernels: 68.5 us -> 62 us
  local copies, waits for them, and re-layouts: 2.22 us -> 1.28 us
    pallas_call x1, Pallas kernels: 68.5 us -> 62 us  [local(): pl.pallas_call(kernel, out_shape=(out, out), in_specs=[pl.BlockSpec(memor...]
    unnamed x4 -> x2, local copies, waits for them, and re-layouts: 2.22 us -> 1.28 us
where the time goes in v3:
time: 65.2 us; the launch traced here: 63.9 us
  Pallas kernels  62 us (95%)
  local copies, waits for them, and re-layouts  1.28 us (2%)
    pallas_call x1, Pallas kernels, local(): pl.pallas_call(kernel, out_shape=(out, out), in_specs=[pl.BlockSpec(memor...  62 us

profile of v3, /device:TPU:1, one launch (start us, length us, event | category | flops | bytes accessed | tf_op | source)
XLA Modules:
  0.0 63.9 jit_solution(7513250398036448019)
XLA Ops:
  0.6 62.0 %contrastive.1 = (f32[20,1024]{1,0:T(8,128)S(1)}, f32[20,1024]{1,0:T(8,128)S(1)}) custom-call(bf16[20,1024]{1,0:T(8,128)(2,1)} %is_hbm.1, bf16[20,1024]{1,0:T(8,128)(2,1)} %cs_hbm.1, bf16[20,768]{1,0:T(8,128)(2,1)} %it_hbm.1, bf16[20,768]{1,0:T(8,128)(2,1)} %ct_hbm.1), custom_call_target="tpu_custom_call" | custom-call | flops 1600000000 | bytes 400000 | tf_op jit(solution)/shard_map/contrastive/pallas_call | solution.py:435
  62.6 0.6 %copy.8 = f32[20,1024]{1,0:T(8,128)} copy(f32[20,1024]{1,0:T(8,128)S(1)} %get-tuple-element.2) | data formatting | bytes 163840
  63.3 0.6 %copy.9 = f32[20,1024]{1,0:T(8,128)} copy(f32[20,1024]{1,0:T(8,128)S(1)} %get-tuple-element.3) | data formatting | bytes 163840

commit v4 on v0

v4 whole, which is shorter than its diff:
```python
import math

import jax
import jax.numpy as jnp
from jax import lax
from jax.experimental import pallas as pl
from jax.experimental.pallas import tpu as pltpu
from jax.sharding import PartitionSpec as P

MESH = pl.DeviceIdType.MESH
GAIN = 3.0
NX, NYH, NZ = 4, 4, 8
NR = NQ = 16
DS, DT = 1024, 768
W = 256 + DS
WIDTH = (256 + DS, 256 + DT)
B = 20
MAIN, M = 32 * NR, 40 * NR
BF, F32 = jnp.bfloat16, jnp.float32
ORDER = "P0U1D1L0R0Y1Y3E1F1X0U2D2L1R1Y2E2L3R3F2U3D3X1R2L2E3F3X3U4X2F4"


def dot_t(a, b):
    return lax.dot_general(a, b, (((1,), (1,)), ((), ())), preferred_element_type=F32)


def t_dot(a, b):
    return lax.dot_general(a, b, (((0,), (0,)), ((), ())), preferred_element_type=F32)


def dot(a, b):
    return jnp.dot(a, b, preferred_element_type=F32)


def fold_matrix():
    a = lax.broadcasted_iota(jnp.int32, (256, 256), 0)
    b = lax.broadcasted_iota(jnp.int32, (256, 256), 1)
    source = 16 * ((a >> 2) & 15) + 4 * (a >> 6) + (a & 3)
    return jnp.where(b == source, 1.0, 0.0).astype(BF)


def pool(parts):
    m = jnp.max(parts, axis=0)
    return m + jnp.log(jnp.sum(jnp.exp(parts - m[None]), axis=0))


def kernel(
    is_hbm, cs_hbm, it_hbm, ct_hbm, oi_ref, oc_ref,
    is_ref, cs_ref, it_ref, ct_ref, rp, pk, gi, gc, ar, br, gcs, brs,
    sb, er, ec, rmx, cmx, tb, tb2, rxr, rxc, tg,
    pg, sg, s_p, r_p, s_z, r_z, s_x, r_x, s_y, r_y, own_i, own_c, o_s,
    in_sem, sib_r, sib_s, gi_r, gc_r, first_s, next_s, ex_r, ex_s, lr_r, lr_s, lc_r, lc_s,
    p_r, p_s, z_r, z_s, x_r, x_s, y_r, y_s, o_r, o_send,
):
    img, cap = lax.axis_index("img"), lax.axis_index("cap")
    yh, x, core = img // (2 * NX), (img // 2) % NX, img % 2
    yl, z = cap // NZ, cap % NZ

    def at_img(dyh, dx):
        return (((yh + dyh) % NYH) * NX + (x + dx) % NX) * 2

    def slot_c(dyh, dx):
        return ((yh + dyh) % NYH) * NX + (x + dx) % NX

    def at_cap(dyl, dz):
        return ((yl + dyl) % 2) * NZ + (z + dz) % NZ

    def rows(slot, n):
        return pl.ds(pl.multiple_of(n * slot, n), n)

    def remote(src, dst, send, recv, dev):
        return pltpu.make_async_remote_copy(
            src_ref=src, dst_ref=dst, send_sem=send, recv_sem=recv, device_id=dev, device_id_type=MESH
        )

    def push(src, dst, send, recv, dev):
        remote(src, dst, send, recv, dev).start()

    def sent(ref, sem):
        remote(ref, ref, sem, in_sem.at[0], sib).wait_send()

    up, down, pair = (img, at_cap(0, 1)), (img, at_cap(0, -1)), (img, at_cap(1, 0))
    xu, xd, x2 = [(at_img(0, d) + core, cap) for d in (1, -1, 2)]
    ys = [(at_img(d, 0) + core, cap) for d in (1, 2, 3)]
    sib = (at_img(0, 0) + 1 - core, cap)

    def arrived(ref, sem):
        remote(ref, ref, in_sem.at[0], sem, sib).wait_recv()

    barrier = pltpu.get_barrier_semaphore()
    chip = at_img(0, 0)
    around_i = [(chip, at_cap(1, 0)), (chip, at_cap(0, 1)), (chip, at_cap(0, -1))]
    around_c = [(at_img(*d), cap) for d in ((2, 0), (1, 0), (3, 0), (0, 1), (0, -1))]
    near = [sib] + [(dev[0] + c, dev[1]) for dev in around_i + around_c for c in range(2)]
    for dev in near:
        pl.semaphore_signal(barrier, inc=1, device_id=dev, device_id_type=MESH)

    loads = []
    for n, (src, dst) in enumerate(((is_hbm, is_ref), (it_hbm, it_ref), (cs_hbm, cs_ref), (ct_hbm, ct_ref))):
        c = pltpu.make_async_copy(src, dst, in_sem.at[n])
        c.start()
        loads.append(c)
    for c in loads:
        c.wait()

    for n, (k, j, src, width) in enumerate(
        ((0, 0, is_ref, DS), (1, 0, it_ref, DT), (0, 1, cs_ref, DS), (1, 1, ct_ref, DT))
    ):
        pk[k, j, :, 256 : 256 + width] = src[0:16, :]
        if width < DS:
            pk[k, j, :, 256 + width : W] = jnp.zeros((16, DS - width), BF)
        last = src[...].astype(F32)[16:20, :]
        rp[n] = jnp.zeros((16, 256), F32)
        for q in range(width // 256):
            rp[n, 4 * q : 4 * q + 4, :] = last[:, 256 * q : 256 * q + 256]
        pk[k, j, :, 0:256] = rp[n].astype(BF)

    @pl.when(core == 1)
    def _():
        gi[:, 256 + DT : W] = jnp.zeros((MAIN, DS - DT), BF)
        gc[:, 256 + DT : W] = jnp.zeros((MAIN, DS - DT), BF)

    pl.semaphore_wait(barrier, len(near))

    me_i, me_c = cap, slot_c(0, 0)
    mine_i, mine_c = rows(2 * me_i + core, 16), rows(2 * me_c + core, 16)
    for k, width in enumerate(WIDTH):

        @pl.when(core != k)
        def _():
            w = pl.ds(0, width)
            push(pk.at[k, 0, :, w], gi.at[mine_i, w], sib_s.at[0], sib_r.at[0], sib)
            push(pk.at[k, 1, :, w], gc.at[mine_c, w], sib_s.at[1], sib_r.at[1], sib)

    for dev in around_i:
        for k, width in enumerate(WIDTH):
            w = pl.ds(0, width)
            push(pk.at[k, 0, :, w], gi.at[mine_i, w], first_s.at[k], gi_r.at[me_i], (dev[0] + k, dev[1]))
    for dev in around_c:
        for k, width in enumerate(WIDTH):
            w = pl.ds(0, width)
            push(pk.at[k, 1, :, w], gc.at[mine_c, w], first_s.at[k], gc_r.at[me_c], (dev[0] + k, dev[1]))
    gi[mine_i, :] = pk[core, 0]
    gc[mine_c, :] = pk[core, 1]

    flow = {}
    for k in (1, 2, 3):
        flow["U%d" % k] = (at_cap(0, -k), (up,))
        flow["D%d" % k] = (at_cap(0, k), (down,) if k < 3 else ())
        flow["E%d" % k] = (at_cap(1, -k), (up,) if k < 3 else ())
        flow["F%d" % k] = (at_cap(1, k), (down,))
    flow["P0"] = (at_cap(1, 0), (up, down))
    flow["U4"] = (at_cap(0, -4), ())
    flow["F4"] = (at_cap(1, 4), ())
    for j in range(NYH):
        if j:
            flow["Y%d" % j] = (slot_c(j, 0), (xu, xd))
        flow["L%d" % j] = (slot_c(j, -1), (xu,) if j < 2 else ())
        flow["R%d" % j] = (slot_c(j, 1), (xd,) if j >= 2 else ())
        flow["X%d" % j] = (slot_c(j, 2), ())

    for k, width in enumerate(WIDTH):

        @pl.when(core == k)
        def _():
            for n in range(0, len(ORDER), 2):
                name = ORDER[n : n + 2]
                slot, devs = flow[name]
                buf, recv, send = (gc, gc_r, next_s.at[1]) if name[0] in "YLRX" else (gi, gi_r, next_s.at[0])
                block = buf.at[rows(slot, 32), pl.ds(0, width)]
                arrived(block, recv.at[slot])
                for dev in devs:
                    push(block, block, send, recv.at[slot], dev)
            arrived(gi.at[rows(2 * me_i + 1 - core, 16), pl.ds(0, width)], sib_r.at[0])
            arrived(gc.at[rows(2 * me_c + 1 - core, 16), pl.ds(0, width)], sib_r.at[1])

    @pl.when(core == 0)
    def _():
        push(gc.at[:, pl.ds(256, DS)], gcs, ex_s.at[1], ex_r.at[1], sib)

    fold = fold_matrix()
    for src, dst in ((gi, ar), (gc, br)):
        for h in range(2):
            y = dot(fold, src[256 * h : 256 * h + 256, 0:256]).astype(BF)
            for q in range(4):
                dst[64 * h : 64 * h + 64, 256 * q : 256 * q + 256] = y[64 * q : 64 * q + 64, :]

    @pl.when(core == 0)
    def _():
        push(br, brs, ex_s.at[2], ex_r.at[2], sib)

    gain = jnp.where(core == 0, GAIN / math.sqrt(DS), GAIN / math.sqrt(DT))
    sb[core, 0:MAIN, 0:MAIN] = gain * dot_t(gi[:, 256:W], gc[:, 256:W])
    sb[core, 0:MAIN, MAIN:M] = gain * dot_t(gi[:, 256:W], br[...])
    sb[core, MAIN:M, 0:MAIN] = gain * dot_t(ar[...], gc[:, 256:W])
    sb[core, MAIN:M, MAIN:M] = gain * dot_t(ar[...], br[...])
    push(sb.at[core], sb.at[core], ex_s.at[0], ex_r.at[0], sib)

    def statistics(k):
        top, total, lses = None, None, []
        for b in range(0, M, 64):
            blk = sb[k, b : b + 64, :]
            m = jnp.max(blk, axis=1, keepdims=True)
            rmx[k, b : b + 64, :] = m
            e = jnp.exp(blk - m)
            er[k, b : b + 64, :] = e
            lses.append(m + jnp.log(jnp.sum(e, axis=1, keepdims=True)))
            t = jnp.max(blk, axis=0, keepdims=True)
            top = t if top is None else jnp.maximum(top, t)
        for b in range(0, M, 64):
            e = jnp.exp(sb[k, b : b + 64, :] - top)
            ec[k, b : b + 64, :] = e
            t = jnp.sum(e, axis=0, keepdims=True)
            total = t if total is None else total + t
        cmx[k] = top
        return lses, top + jnp.log(total)

    row_lse, col_lse = statistics(core)

    rxc[core * NQ + me_c] = col_lse
    for n, b in enumerate(range(0, M, 64)):
        tb[b : b + 64, :] = jnp.broadcast_to(row_lse[n], (64, 128))
    rxr[core * NR + me_i] = tb[...].T[0:1, :]
    mine = rxc.at[core * NQ + me_c]
    for j in (2, 1, 3, 0):
        for dx in (2, 1, 3, 0):
            if (j, dx) != (0, 0):
                for c in range(2):
                    push(mine, mine, lc_s.at[0], lc_r.at[core], (at_img(j, dx) + c, cap))
    push(mine, mine, lc_s.at[0], lc_r.at[core], sib)
    mine = rxr.at[core * NR + me_i]
    for dz in (4, 3, 5, 2, 6, 1, 7, 0):
        for dy in (1, 0):
            if (dy, dz) != (0, 0):
                for c in range(2):
                    push(mine, mine, lr_s.at[0], lr_r.at[core], (chip + c, at_cap(dy, dz)))
    push(mine, mine, lr_s.at[0], lr_r.at[core], sib)

    tb2[...] = jnp.zeros_like(tb2)
    for k, width in enumerate(WIDTH):
        sent(gi.at[pl.ds(0, 128), pl.ds(0, width)], first_s.at[k])

        @pl.when(core == k)
        def _():
            sent(gi.at[pl.ds(0, 384), pl.ds(0, width)], next_s.at[0])
            sent(gc.at[pl.ds(0, 320), pl.ds(0, width)], next_s.at[1])

        @pl.when(core != k)
        def _():
            for n in range(2):
                sent(gi.at[pl.ds(0, 16), pl.ds(0, width)], sib_s.at[n])

    arrived(sb.at[1 - core], ex_r.at[0])
    statistics(1 - core)

    arrived(rxc.at[pl.ds(0, NQ - 1)], lc_r.at[core])
    arrived(rxc.at[pl.ds(0, NQ)], lc_r.at[1 - core])
    arrived(rxr.at[pl.ds(0, NR - 1)], lr_r.at[core])
    arrived(rxr.at[pl.ds(0, NR)], lr_r.at[1 - core])
    tb2[0:1, :] = pool(rxr[0:NR])
    tb2[1:2, :] = pool(rxr[NR : 2 * NR])
    rows_all = tb2[...].T
    f_col_s = 0.5 * jnp.exp(cmx[0] - pool(rxc[0:NQ]))
    f_col_t = 0.25 * jnp.exp(cmx[1] - pool(rxc[NQ : 2 * NQ]))

    b = lax.broadcasted_iota(jnp.int32, (1, M), 1)
    t = jnp.where(b < MAIN, b >> 4, (b - MAIN) >> 2)
    u = jnp.where(b < MAIN, b & 15, 16 + (b & 3))
    col_id = cap * M + t * B + u
    for lo in range(0, M, 64):
        a = lo + lax.broadcasted_iota(jnp.int32, (64, 1), 0)
        t, u = (a >> 4, a & 15) if lo < MAIN else ((a - MAIN) >> 2, 16 + (a & 3))
        row_id = (at_img(0, 0) + (t & 1)) * (B * NR) + (t >> 1) * B + u
        here = slice(lo, lo + 64)
        f_row_s = 0.5 * jnp.exp(rmx[0, here, :] - rows_all[here, 0:1])
        f_row_t = 0.25 * jnp.exp(rmx[1, here, :] - rows_all[here, 1:2])
        g = er[0, here, :] * f_row_s + ec[0, here, :] * f_col_s
        g = g - (er[1, here, :] * f_row_t + ec[1, here, :] * f_col_t)
        g = g - jnp.where(row_id == col_id, 0.5, 0.0)
        tg[here, :] = g.astype(BF)

    def folded(v):
        v = jnp.concatenate([v[:, 256 * q : 256 * q + 256] for q in range(4)], axis=0)
        hi = v.astype(BF)
        lo = (v - hi.astype(F32)).astype(BF)
        return t_dot(fold, hi) + t_dot(fold, lo)

    def as_blocks():
        for h in range(2):
            here = slice(256 * h, 256 * h + 256)
            sg[here, 0:DS] = pg[here, :]
            sg[here, DS:W] = folded(pg[MAIN + 64 * h : MAIN + 64 * h + 64, :])

    def unfold(acc, out):
        out[0:16, :] = acc[:, 0:DS]
        for q in range(4):
            out[16:20, 256 * q : 256 * q + 256] = acc[4 * q : 4 * q + 4, DS:W]

    def finish():
        arrived(r_y, y_r.at[0])
        acc = own_c[...]
        for n in range(3):
            acc = acc + r_y[n].astype(F32)
        unfold(acc, oc_ref)
        arrived(r_z.at[pl.ds(0, NZ - 1)], z_r.at[0])
        r_z[z] = jnp.zeros((16, W), BF)
        acc = own_i[...]
        for n in range(NZ):
            acc = acc + r_z[n].astype(F32)
        unfold(acc, oi_ref)

    def drain():
        sent(sb.at[0], ex_s.at[0])
        sent(rxr.at[pl.ds(0, 2 * NR - 1)], lr_s.at[0])
        sent(rxc.at[pl.ds(0, 2 * NQ - 1)], lc_s.at[0])

    @pl.when(core == 0)
    def _():
        pg[...] = t_dot(tg[0:MAIN, :], gi[:, 256:W]) + t_dot(tg[MAIN:M, :], ar[...])
        as_blocks()
        order_y = (2, 1, 3, 0)
        for n, d in enumerate(order_y):
            s_x[n] = sg[rows((yh + d) % NYH, 32 * NX), :].astype(BF)
            for k, (dx, dev) in enumerate(((2, x2), (1, xu), (3, xd))):
                push(s_x.at[n, rows((x + dx) % NX, 32), :], r_x.at[3 * n + k], x_s.at[0], x_r.at[n], dev)
        drain()
        sent(gcs, ex_s.at[1])
        sent(brs, ex_s.at[2])
        for n, d in enumerate(order_y):
            v = sg[rows(slot_c(d, 0), 32), :]
            arrived(r_x.at[pl.ds(3 * n, 3)], x_r.at[n])
            for k in range(3):
                v = v + r_x[3 * n + k].astype(F32)
            if d:
                s_y[n] = v.astype(BF)
                for c in range(2):
                    push(s_y.at[n, pl.ds(16 * c, 16), :], r_y.at[n], y_s.at[0], y_r.at[0], (at_img(d, 0) + c, cap))
            else:
                own_c[...] = v[0:16, :]
                o_s[...] = v[16:32, :]
                push(o_s, own_c, o_send.at[0], o_r.at[0], sib)
        sent(r_x, x_s.at[0])
        arrived(own_i, o_r.at[0])
        finish()
        sent(s_y, y_s.at[0])
        sent(o_s, o_send.at[0])

    @pl.when(core == 1)
    def _():
        arrived(gcs, ex_r.at[1])
        arrived(brs, ex_r.at[2])
        pg[...] = dot(tg[:, 0:MAIN], gcs[...]) + dot(tg[:, MAIN:M], brs[...])
        as_blocks()
        for n in range(NZ):
            s_p[n] = sg[rows((1 - yl) * NZ + n, 32), :].astype(BF)
            push(s_p.at[n], r_p.at[n], p_s.at[0], p_r.at[n], pair)
        drain()
        for n in range(NZ):
            arrived(r_p.at[n], p_r.at[n])
            v = sg[rows(yl * NZ + n, 32), :] + r_p[n].astype(F32)
            s_z[n] = v.astype(BF)

            @pl.when(z != n)
            def _():
                for c in range(2):
                    push(s_z.at[n, pl.ds(16 * c, 16), :], r_z.at[z], z_s.at[0], z_r.at[0], (chip + c, yl * NZ + n))

            @pl.when(z == n)
            def _():
                own_i[...] = v[16:32, :]
                o_s[...] = v[0:16, :]
                push(o_s, own_i, o_send.at[0], o_r.at[0], sib)

        sent(s_p, p_s.at[0])
        arrived(own_c, o_r.at[0])
        finish()
        sent(s_z.at[pl.ds(0, NZ - 1)], z_s.at[0])
        sent(o_s, o_send.at[0])


def local(image_student, caption_student, image_teacher, caption_teacher):
    vmem = pl.BlockSpec(memory_space=pltpu.VMEM)
    dma = pltpu.SemaphoreType.DMA
    out = pltpu.VMEM((B, DS), F32)
    args = [
        pltpu.with_memory_space_constraint(a, pltpu.HBM)
        for a in (image_student, caption_student, image_teacher, caption_teacher)
    ]
    return pl.pallas_call(
        kernel,
        out_shape=(out, out),
        in_specs=[pl.BlockSpec(memory_space=pltpu.HBM)] * 4,
        out_specs=(vmem, vmem),
        scratch_shapes=[
            pltpu.VMEM((B, DS), BF),
            pltpu.VMEM((B, DS), BF),
            pltpu.VMEM((B, DT), BF),
            pltpu.VMEM((B, DT), BF),
            pltpu.VMEM((4, 16, 256), F32),
            pltpu.VMEM((2, 2, 16, W), BF),
            pltpu.VMEM((MAIN, W), BF),
            pltpu.VMEM((MAIN, W), BF),
            pltpu.VMEM((M - MAIN, DS), BF),
            pltpu.VMEM((M - MAIN, DS), BF),
            pltpu.VMEM((MAIN, DS), BF),
            pltpu.VMEM((M - MAIN, DS), BF),
            pltpu.VMEM((2, M, M), F32),
            pltpu.VMEM((2, M, M), F32),
            pltpu.VMEM((2, M, M), F32),
            pltpu.VMEM((2, M, 1), F32),
            pltpu.VMEM((2, 1, M), F32),
            pltpu.VMEM((M, 128), F32),
            pltpu.VMEM((128, M), F32),
            pltpu.VMEM((2 * NR, 1, M), F32),
            pltpu.VMEM((2 * NQ, 1, M), F32),
            pltpu.VMEM((M, M), BF),
            pltpu.VMEM((M, DS), F32),
            pltpu.VMEM((MAIN, W), F32),
            pltpu.VMEM((NZ, 32, W), BF),
            pltpu.VMEM((NZ, 32, W), BF),
            pltpu.VMEM((NZ, 32, W), BF),
            pltpu.VMEM((NZ, 16, W), BF),
            pltpu.VMEM((NYH, 32 * NX, W), BF),
            pltpu.VMEM((3 * NYH, 32, W), BF),
            pltpu.VMEM((3, 32, W), BF),
            pltpu.VMEM((3, 16, W), BF),
            pltpu.VMEM((16, W), F32),
            pltpu.VMEM((16, W), F32),
            pltpu.VMEM((16, W), F32),
            dma((4,)), dma((2,)), dma((2,)), dma((NR,)), dma((NQ,)), dma((2,)), dma((2,)),
            dma((3,)), dma((3,)), dma((2,)), dma((1,)), dma((2,)), dma((1,)),
            dma((NZ,)), dma((1,)), dma((1,)), dma((1,)),
            dma((NYH,)), dma((1,)), dma((1,)), dma((1,)), dma((1,)), dma((1,)),
        ],
        compiler_params=pltpu.CompilerParams(
            collective_id=0, has_side_effects=True, vmem_limit_bytes=56 * 2**20
        ),
        cost_estimate=pl.CostEstimate(flops=1_800_000_000, bytes_accessed=400_000, transcendentals=1_700_000),
        name="contrastive",
    )(*args)


def solution(mesh):
    return jax.shard_map(
        local,
        mesh=mesh,
        in_specs=(
            P(("img", "cap"), None),
            P(("cap", "img"), None),
            P(("img", "cap"), None),
            P(("cap", "img"), None),
        ),
        out_specs=(P(("img", "cap"), None), P(("cap", "img"), None)),
        check_vma=False,
    )
```

time: 530 us -> 66.8 us (0.13); the launches traced: 521 us -> 66.3 us
  blocking collectives: 460 us -> 0 us
  Pallas kernels: 0 us -> 64.4 us
  starting transfers between devices: 25 us -> 0 us
  between operations: 15.6 us -> 0.64 us
  local copies, waits for them, and re-layouts: 10.2 us -> 1.28 us
    unnamed x2 -> x0, blocking collectives: 133 us -> none
    all_gather x3 -> x0, blocking collectives: 123 us -> none  [the longest x1 58.1 us: local(): lax.all_gather(caption_teacher, 'img', axis=0, tiled=True)]
    pmax x2 -> x0, blocking collectives: 102 us -> none  [the longest x1 76.9 us: column_pool(): peak_s, peak_t = lax.pmax((parts[0], parts[2]), 'img')]
    psum x2 -> x0, blocking collectives: 102 us -> none  [the longest x1 77.9 us: column_pool(): lax.psum((parts[1] * jnp.exp(parts[0] - peak_s), parts[3] * jnp.exp(parts...]
    pallas_call x0 -> x1, Pallas kernels: none -> 64.4 us  [local(): pl.pallas_call(kernel, out_shape=(out, out), in_specs=[pl.BlockSpec(memor...]
    unnamed x9 -> x0, starting transfers between devices: 25 us -> none
    unnamed x20 -> x2, local copies, waits for them, and re-layouts: 10.2 us -> 1.28 us
  transfers between devices with their start and end apart: 10 -> 0, of which waited for: 1 -> 0; matrix products, arithmetic and copies ran while one was open for 21% -> 0% of each run, Pallas kernels for 0% -> 0%
where the time goes in v4:
time: 66.8 us; the launch traced here: 66.3 us
  Pallas kernels  64.4 us (96%)
  local copies, waits for them, and re-layouts  1.28 us (2%)
    pallas_call x1, Pallas kernels, local(): pl.pallas_call(kernel, out_shape=(out, out), in_specs=[pl.BlockSpec(memor...  64.4 us

profile of v4, /device:TPU:1, one launch (start us, length us, event | category | flops | bytes accessed | tf_op | source)
XLA Modules:
  0.0 66.3 jit_solution(4158385292413024535)
XLA Ops:
  0.6 64.4 %contrastive.1 = (f32[20,1024]{1,0:T(8,128)S(1)}, f32[20,1024]{1,0:T(8,128)S(1)}) custom-call(bf16[20,1024]{1,0:T(8,128)(2,1)} %is_hbm.1, bf16[20,1024]{1,0:T(8,128)(2,1)} %cs_hbm.1, bf16[20,768]{1,0:T(8,128)(2,1)} %it_hbm.1, bf16[20,768]{1,0:T(8,128)(2,1)} %ct_hbm.1), custom_call_target="tpu_custom_call" | custom-call | flops 1800000000 | bytes 400000 | tf_op jit(solution)/shard_map/contrastive/pallas_call | solution.py:389
  65.0 0.6 copy.8
  65.7 0.6 copy.9

commit v5 on v4

--- a/solution.py
+++ b/solution.py
@@ -17,7 +17,7 @@
 B = 20
 MAIN, M = 32 * NR, 40 * NR
 BF, F32 = jnp.bfloat16, jnp.float32
-ORDER = "P0U1D1L0R0Y1Y3E1F1X0U2D2L1R1Y2E2L3R3F2U3D3X1R2L2E3F3X3U4X2F4"
+ORDER = "P0U1D1L0R0Y1Y3E1F1U2D2X0L1R1Y2E2F2L3R3U3D3X1R2L2E3F3X3U4X2F4"
 
 
 def dot_t(a, b):
@@ -48,7 +48,7 @@
     is_hbm, cs_hbm, it_hbm, ct_hbm, oi_ref, oc_ref,
     is_ref, cs_ref, it_ref, ct_ref, rp, pk, gi, gc, ar, br, gcs, brs,
     sb, er, ec, rmx, cmx, tb, tb2, rxr, rxc, tg,
-    pg, sg, s_p, r_p, s_z, r_z, s_x, r_x, s_y, r_y, own_i, own_c, o_s,
+    sg, s_p, r_p, s_z, r_z, s_x, r_x, s_y, r_y, own_i, own_c, o_s,
     in_sem, sib_r, sib_s, gi_r, gc_r, first_s, next_s, ex_r, ex_s, lr_r, lr_s, lc_r, lc_s,
     p_r, p_s, z_r, z_s, x_r, x_s, y_r, y_s, o_r, o_send,
 ):
@@ -136,10 +136,14 @@
         for k, width in enumerate(WIDTH):
             w = pl.ds(0, width)
             push(pk.at[k, 0, :, w], gi.at[mine_i, w], first_s.at[k], gi_r.at[me_i], (dev[0] + k, dev[1]))
-    for dev in around_c:
+
+    def own_caption(dev):
         for k, width in enumerate(WIDTH):
             w = pl.ds(0, width)
             push(pk.at[k, 1, :, w], gc.at[mine_c, w], first_s.at[k], gc_r.at[me_c], (dev[0] + k, dev[1]))
+
+    for dev in around_c[3:] + around_c[1:3]:
+        own_caption(dev)
     gi[mine_i, :] = pk[core, 0]
     gc[mine_c, :] = pk[core, 1]
 
@@ -159,24 +163,31 @@
         flow["R%d" % j] = (slot_c(j, 1), (xd,) if j >= 2 else ())
         flow["X%d" % j] = (slot_c(j, 2), ())
 
+    def caption(slot):
+        push(gc.at[rows(slot, 32), pl.ds(256, DS)], gcs.at[rows(slot, 32), :], ex_s.at[1], ex_r.at[1], sib)
+
     for k, width in enumerate(WIDTH):
 
         @pl.when(core == k)
         def _():
             for n in range(0, len(ORDER), 2):
                 name = ORDER[n : n + 2]
+                if n == 6:
+                    own_caption(around_c[0])
+                    arrived(gi.at[rows(2 * me_i + 1 - core, 16), pl.ds(0, width)], sib_r.at[0])
+                    arrived(gc.at[rows(2 * me_c + 1 - core, 16), pl.ds(0, width)], sib_r.at[1])
                 slot, devs = flow[name]
                 buf, recv, send = (gc, gc_r, next_s.at[1]) if name[0] in "YLRX" else (gi, gi_r, next_s.at[0])
                 block = buf.at[rows(slot, 32), pl.ds(0, width)]
                 arrived(block, recv.at[slot])
                 for dev in devs:
                     push(block, block, send, recv.at[slot], dev)
-            arrived(gi.at[rows(2 * me_i + 1 - core, 16), pl.ds(0, width)], sib_r.at[0])
-            arrived(gc.at[rows(2 * me_c + 1 - core, 16), pl.ds(0, width)], sib_r.at[1])
-
-    @pl.when(core == 0)
-    def _():
-        push(gc.at[:, pl.ds(256, DS)], gcs, ex_s.at[1], ex_r.at[1], sib)
+                if k == 0 and n == len(ORDER) - 12:
+                    for j in range(NYH):
+                        for d in (0, 1, 3) if j > 1 else range(NX):
+                            caption(slot_c(j, d))
+                if k == 0 and name[0] == "X" and n > len(ORDER) - 12:
+                    caption(slot)
 
     fold = fold_matrix()
     for src, dst in ((gi, ar), (gc, br)):
@@ -221,20 +232,18 @@
     for n, b in enumerate(range(0, M, 64)):
         tb[b : b + 64, :] = jnp.broadcast_to(row_lse[n], (64, 128))
     rxr[core * NR + me_i] = tb[...].T[0:1, :]
-    mine = rxc.at[core * NQ + me_c]
-    for j in (2, 1, 3, 0):
-        for dx in (2, 1, 3, 0):
-            if (j, dx) != (0, 0):
-                for c in range(2):
-                    push(mine, mine, lc_s.at[0], lc_r.at[core], (at_img(j, dx) + c, cap))
-    push(mine, mine, lc_s.at[0], lc_r.at[core], sib)
-    mine = rxr.at[core * NR + me_i]
-    for dz in (4, 3, 5, 2, 6, 1, 7, 0):
-        for dy in (1, 0):
-            if (dy, dz) != (0, 0):
-                for c in range(2):
-                    push(mine, mine, lr_s.at[0], lr_r.at[core], (chip + c, at_cap(dy, dz)))
-    push(mine, mine, lr_s.at[0], lr_r.at[core], sib)
+    mine_c, mine_r = rxc.at[core * NQ + me_c], rxr.at[core * NR + me_i]
+    far = [(2 * min(j, 4 - j) + min(d, 4 - d), j, d, True) for j in range(NYH) for d in range(NX)]
+    far += [(j + min(d, 8 - d), j, d, False) for j in range(2) for d in range(NZ)]
+    for hops, j, d, of_columns in sorted(far, reverse=True):
+        if hops:
+            for c in range(2):
+                if of_columns:
+                    push(mine_c, mine_c, lc_s.at[0], lc_r.at[core], (at_img(j, d) + c, cap))
+                else:
+                    push(mine_r, mine_r, lr_s.at[0], lr_r.at[core], (chip + c, at_cap(j, d)))
+    push(mine_c, mine_c, lc_s.at[0], lc_r.at[core], sib)
+    push(mine_r, mine_r, lr_s.at[0], lr_r.at[core], sib)
 
     tb2[...] = jnp.zeros_like(tb2)
     for k, width in enumerate(WIDTH):
@@ -285,12 +294,6 @@
         lo = (v - hi.astype(F32)).astype(BF)
         return t_dot(fold, hi) + t_dot(fold, lo)
 
-    def as_blocks():
-        for h in range(2):
-            here = slice(256 * h, 256 * h + 256)
-            sg[here, 0:DS] = pg[here, :]
-            sg[here, DS:W] = folded(pg[MAIN + 64 * h : MAIN + 64 * h + 64, :])
-
     def unfold(acc, out):
         out[0:16, :] = acc[:, 0:DS]
         for q in range(4):
@@ -316,11 +319,14 @@
 
     @pl.when(core == 0)
     def _():
-        pg[...] = t_dot(tg[0:MAIN, :], gi[:, 256:W]) + t_dot(tg[MAIN:M, :], ar[...])
-        as_blocks()
+        last = t_dot(tg[0:MAIN, MAIN:M], gi[:, 256:W]) + t_dot(tg[MAIN:M, MAIN:M], ar[...])
+        for h in range(2):
+            sg[256 * h : 256 * h + 256, DS:W] = folded(last[64 * h : 64 * h + 64, :])
         order_y = (2, 1, 3, 0)
         for n, d in enumerate(order_y):
-            s_x[n] = sg[rows((yh + d) % NYH, 32 * NX), :].astype(BF)
+            group = rows((yh + d) % NYH, 32 * NX)
+            sg[group, 0:DS] = t_dot(tg[0:MAIN, group], gi[:, 256:W]) + t_dot(tg[MAIN:M, group], ar[...])
+            s_x[n] = sg[group, :].astype(BF)
             for k, (dx, dev) in enumerate(((2, x2), (1, xu), (3, xd))):
                 push(s_x.at[n, rows((x + dx) % NX, 32), :], r_x.at[3 * n + k], x_s.at[0], x_r.at[n], dev)
         drain()
@@ -349,11 +355,16 @@
     def _():
         arrived(gcs, ex_r.at[1])
         arrived(brs, ex_r.at[2])
-        pg[...] = dot(tg[:, 0:MAIN], gcs[...]) + dot(tg[:, MAIN:M], brs[...])
-        as_blocks()
-        for n in range(NZ):
-            s_p[n] = sg[rows((1 - yl) * NZ + n, 32), :].astype(BF)
-            push(s_p.at[n], r_p.at[n], p_s.at[0], p_r.at[n], pair)
+        last = dot(tg[MAIN:M, 0:MAIN], gcs[...]) + dot(tg[MAIN:M, MAIN:M], brs[...])
+        for h in range(2):
+            sg[256 * h : 256 * h + 256, DS:W] = folded(last[64 * h : 64 * h + 64, :])
+        for m in range(4):
+            group = rows(2 * ((1 - yl) if m < 2 else yl) + m % 2, 128)
+            sg[group, 0:DS] = dot(tg[group, 0:MAIN], gcs[...]) + dot(tg[group, MAIN:M], brs[...])
+            if m < 2:
+                for n in range(4 * m, 4 * m + 4):
+                    s_p[n] = sg[rows((1 - yl) * NZ + n, 32), :].astype(BF)
+                    push(s_p.at[n], r_p.at[n], p_s.at[0], p_r.at[n], pair)
         drain()
         for n in range(NZ):
             arrived(r_p.at[n], p_r.at[n])
@@ -414,7 +425,6 @@
             pltpu.VMEM((2 * NR, 1, M), F32),
             pltpu.VMEM((2 * NQ, 1, M), F32),
             pltpu.VMEM((M, M), BF),
-            pltpu.VMEM((M, DS), F32),
             pltpu.VMEM((MAIN, W), F32),
             pltpu.VMEM((NZ, 32, W), BF),
             pltpu.VMEM((NZ, 32, W), BF),

time: 66.8 us -> 62.4 us (0.934)
  Pallas kernels: 64.4 us -> 60 us
    pallas_call x1, Pallas kernels: 64.4 us -> 60 us  [local(): pl.pallas_call(kernel, out_shape=(out, out), in_specs=[pl.BlockSpec(memor...]
where the time goes in v5:
time: 62.4 us; the launch traced here: 61.9 us
  Pallas kernels  60 us (96%)
  local copies, waits for them, and re-layouts  1.28 us (2%)
  between operations  0.64 us (1%)
    pallas_call x1, Pallas kernels, local(): pl.pallas_call(kernel, out_shape=(out, out), in_specs=[pl.BlockSpec(memor...  60 us
    unnamed x2, local copies, waits for them, and re-layouts  1.28 us

profile of v5, /device:TPU:1, one launch (start us, length us, event | category | flops | bytes accessed | tf_op | source)
XLA Modules:
  0.0 61.9 jit_solution(5369354507073022711)
XLA Ops:
  0.6 60.0 %contrastive.1 = (f32[20,1024]{1,0:T(8,128)S(1)}, f32[20,1024]{1,0:T(8,128)S(1)}) custom-call(bf16[20,1024]{1,0:T(8,128)(2,1)} %is_hbm.1, bf16[20,1024]{1,0:T(8,128)(2,1)} %cs_hbm.1, bf16[20,768]{1,0:T(8,128)(2,1)} %it_hbm.1, bf16[20,768]{1,0:T(8,128)(2,1)} %ct_hbm.1), custom_call_target="tpu_custom_call" | custom-call | flops 1800000000 | bytes 400000 | tf_op jit(solution)/shard_map/contrastive/pallas_call | solution.py:400
  60.6 0.6 %copy.8 = f32[20,1024]{1,0:T(8,128)} copy(f32[20,1024]{1,0:T(8,128)S(1)} %get-tuple-element.2) | data formatting | bytes 163840
  61.2 0.6 %copy.9 = f32[20,1024]{1,0:T(8,128)} copy(f32[20,1024]{1,0:T(8,128)S(1)} %get-tuple-element.3) | data formatting | bytes 163840

commit v6 on v5

--- a/solution.py
+++ b/solution.py
@@ -17,6 +17,7 @@
 B = 20
 MAIN, M = 32 * NR, 40 * NR
 BF, F32 = jnp.bfloat16, jnp.float32
+FAR_Z = (4, 3, 5, 2, 6, 1, 7, 0)
 ORDER = "P0U1D1L0R0Y1Y3E1F1U2D2X0L1R1Y2E2F2L3R3U3D3X1R2L2E3F3X3U4X2F4"
 
 
@@ -361,12 +362,14 @@
         for m in range(4):
             group = rows(2 * ((1 - yl) if m < 2 else yl) + m % 2, 128)
             sg[group, 0:DS] = dot(tg[group, 0:MAIN], gcs[...]) + dot(tg[group, MAIN:M], brs[...])
-            if m < 2:
-                for n in range(4 * m, 4 * m + 4):
+            if m == 1:
+                for d in FAR_Z:
+                    n = (z + d) % NZ
                     s_p[n] = sg[rows((1 - yl) * NZ + n, 32), :].astype(BF)
                     push(s_p.at[n], r_p.at[n], p_s.at[0], p_r.at[n], pair)
         drain()
-        for n in range(NZ):
+        for d in FAR_Z:
+            n = (z + d) % NZ
             arrived(r_p.at[n], p_r.at[n])
             v = sg[rows(yl * NZ + n, 32), :] + r_p[n].astype(F32)
             s_z[n] = v.astype(BF)

time: 62.4 us -> 62.1 us (level)
  no operation moved by 1% of the time
where the time goes in v6:
time: 62.1 us; the launch traced here: 61.9 us
  Pallas kernels  60 us (97%)
  local copies, waits for them, and re-layouts  1.28 us (2%)
  between operations  0.64 us (1%)
    pallas_call x1, Pallas kernels, local(): pl.pallas_call(kernel, out_shape=(out, out), in_specs=[pl.BlockSpec(memor...  60 us
    unnamed x2, local copies, waits for them, and re-layouts  1.28 us

profile of v6, /device:TPU:1, one launch (start us, length us, event | category | flops | bytes accessed | tf_op | source)
XLA Modules:
  0.0 61.9 jit_solution(1711785920327996751)
XLA Ops:
  0.6 60.0 %contrastive.1 = (f32[20,1024]{1,0:T(8,128)S(1)}, f32[20,1024]{1,0:T(8,128)S(1)}) custom-call(bf16[20,1024]{1,0:T(8,128)(2,1)} %is_hbm.1, bf16[20,1024]{1,0:T(8,128)(2,1)} %cs_hbm.1, bf16[20,768]{1,0:T(8,128)(2,1)} %it_hbm.1, bf16[20,768]{1,0:T(8,128)(2,1)} %ct_hbm.1), custom_call_target="tpu_custom_call" | custom-call | flops 1800000000 | bytes 400000 | tf_op jit(solution)/shard_map/contrastive/pallas_call | solution.py:403
  60.6 0.6 %copy.8 = f32[20,1024]{1,0:T(8,128)} copy(f32[20,1024]{1,0:T(8,128)S(1)} %get-tuple-element.2) | data formatting | bytes 163840
  61.2 0.6 %copy.9 = f32[20,1024]{1,0:T(8,128)} copy(f32[20,1024]{1,0:T(8,128)S(1)} %get-tuple-element.3) | data formatting | bytes 163840

commit v7 on v6

--- a/solution.py
+++ b/solution.py
@@ -18,7 +18,7 @@
 MAIN, M = 32 * NR, 40 * NR
 BF, F32 = jnp.bfloat16, jnp.float32
 FAR_Z = (4, 3, 5, 2, 6, 1, 7, 0)
-ORDER = "P0U1D1L0R0Y1Y3E1F1U2D2X0L1R1Y2E2F2L3R3U3D3X1R2L2E3F3X3U4X2F4"
+ORDER = "P0U1D1L0R0Y1Y3E1F1X0U2D2L1R1Y2E2L3R3F2U3D3X1R2L2E3F3X3U4X2F4"
 
 
 def dot_t(a, b):
@@ -88,6 +88,12 @@
     def arrived(ref, sem):
         remote(ref, ref, in_sem.at[0], sem, sib).wait_recv()
 
+    loads = []
+    for n, (src, dst) in enumerate(((is_hbm, is_ref), (it_hbm, it_ref), (cs_hbm, cs_ref), (ct_hbm, ct_ref))):
+        c = pltpu.make_async_copy(src, dst, in_sem.at[n])
+        c.start()
+        loads.append(c)
+
     barrier = pltpu.get_barrier_semaphore()
     chip = at_img(0, 0)
     around_i = [(chip, at_cap(1, 0)), (chip, at_cap(0, 1)), (chip, at_cap(0, -1))]
@@ -96,25 +102,20 @@
     for dev in near:
         pl.semaphore_signal(barrier, inc=1, device_id=dev, device_id_type=MESH)
 
-    loads = []
-    for n, (src, dst) in enumerate(((is_hbm, is_ref), (it_hbm, it_ref), (cs_hbm, cs_ref), (ct_hbm, ct_ref))):
-        c = pltpu.make_async_copy(src, dst, in_sem.at[n])
-        c.start()
-        loads.append(c)
-    for c in loads:
-        c.wait()
-
-    for n, (k, j, src, width) in enumerate(
-        ((0, 0, is_ref, DS), (1, 0, it_ref, DT), (0, 1, cs_ref, DS), (1, 1, ct_ref, DT))
-    ):
-        pk[k, j, :, 256 : 256 + width] = src[0:16, :]
-        if width < DS:
-            pk[k, j, :, 256 + width : W] = jnp.zeros((16, DS - width), BF)
-        last = src[...].astype(F32)[16:20, :]
-        rp[n] = jnp.zeros((16, 256), F32)
-        for q in range(width // 256):
-            rp[n, 4 * q : 4 * q + 4, :] = last[:, 256 * q : 256 * q + 256]
-        pk[k, j, :, 0:256] = rp[n].astype(BF)
+    def pack(j):
+        for k, src, width in ((0, (is_ref, cs_ref)[j], DS), (1, (it_ref, ct_ref)[j], DT)):
+            n = 2 * j + k
+            loads[n].wait()
+            pk[k, j, :, 256 : 256 + width] = src[0:16, :]
+            if width < DS:
+                pk[k, j, :, 256 + width : W] = jnp.zeros((16, DS - width), BF)
+            last = src[...].astype(F32)[16:20, :]
+            rp[n] = jnp.zeros((16, 256), F32)
+            for q in range(width // 256):
+                rp[n, 4 * q : 4 * q + 4, :] = last[:, 256 * q : 256 * q + 256]
+            pk[k, j, :, 0:256] = rp[n].astype(BF)
+
+    pack(0)
 
     @pl.when(core == 1)
     def _():
@@ -125,6 +126,20 @@
 
     me_i, me_c = cap, slot_c(0, 0)
     mine_i, mine_c = rows(2 * me_i + core, 16), rows(2 * me_c + core, 16)
+    for dev in around_i:
+        for k, width in enumerate(WIDTH):
+            w = pl.ds(0, width)
+            push(pk.at[k, 0, :, w], gi.at[mine_i, w], first_s.at[k], gi_r.at[me_i], (dev[0] + k, dev[1]))
+
+    pack(1)
+
+    def own_caption(dev):
+        for k, width in enumerate(WIDTH):
+            w = pl.ds(0, width)
+            push(pk.at[k, 1, :, w], gc.at[mine_c, w], first_s.at[k], gc_r.at[me_c], (dev[0] + k, dev[1]))
+
+    for dev in around_c[3:] + around_c[1:3]:
+        own_caption(dev)
     for k, width in enumerate(WIDTH):
 
         @pl.when(core != k)
@@ -133,18 +148,6 @@
             push(pk.at[k, 0, :, w], gi.at[mine_i, w], sib_s.at[0], sib_r.at[0], sib)
             push(pk.at[k, 1, :, w], gc.at[mine_c, w], sib_s.at[1], sib_r.at[1], sib)
 
-    for dev in around_i:
-        for k, width in enumerate(WIDTH):
-            w = pl.ds(0, width)
-            push(pk.at[k, 0, :, w], gi.at[mine_i, w], first_s.at[k], gi_r.at[me_i], (dev[0] + k, dev[1]))
-
-    def own_caption(dev):
-        for k, width in enumerate(WIDTH):
-            w = pl.ds(0, width)
-            push(pk.at[k, 1, :, w], gc.at[mine_c, w], first_s.at[k], gc_r.at[me_c], (dev[0] + k, dev[1]))
-
-    for dev in around_c[3:] + around_c[1:3]:
-        own_caption(dev)
     gi[mine_i, :] = pk[core, 0]
     gc[mine_c, :] = pk[core, 1]
 

time: 62.1 us -> 62.1 us (level)
  no operation moved by 1% of the time
where the time goes in v7:
time: 62.1 us; the launch traced here: 61.9 us
  Pallas kernels  60 us (97%)
  local copies, waits for them, and re-layouts  1.28 us (2%)
  between operations  0.64 us (1%)
    pallas_call x1, Pallas kernels, local(): pl.pallas_call(kernel, out_shape=(out, out), in_specs=[pl.BlockSpec(memor...  60 us
    unnamed x2, local copies, waits for them, and re-layouts  1.28 us

profile of v7, /device:TPU:1, one launch (start us, length us, event | category | flops | bytes accessed | tf_op | source)
XLA Modules:
  0.0 61.9 jit_solution(8645478316139649373)
XLA Ops:
  0.6 60.0 %contrastive.1 = (f32[20,1024]{1,0:T(8,128)S(1)}, f32[20,1024]{1,0:T(8,128)S(1)}) custom-call(bf16[20,1024]{1,0:T(8,128)(2,1)} %is_hbm.1, bf16[20,1024]{1,0:T(8,128)(2,1)} %cs_hbm.1, bf16[20,768]{1,0:T(8,128)(2,1)} %it_hbm.1, bf16[20,768]{1,0:T(8,128)(2,1)} %ct_hbm.1), custom_call_target="tpu_custom_call" | custom-call | flops 1800000000 | bytes 400000 | tf_op jit(solution)/shard_map/contrastive/pallas_call | solution.py:406
  60.6 0.6 %copy.8 = f32[20,1024]{1,0:T(8,128)} copy(f32[20,1024]{1,0:T(8,128)S(1)} %get-tuple-element.2) | data formatting | bytes 163840
  61.2 0.6 %copy.9 = f32[20,1024]{1,0:T(8,128)} copy(f32[20,1024]{1,0:T(8,128)S(1)} %get-tuple-element.3) | data formatting | bytes 163840
